TPU v7x, 128 devices: a whole 4x4x4 slice. The times are simulated.
128 devices in a mesh: section: 2 (over y_lo), tensor: 8 (over x, y_hi), dp: 8 (over z, core).
Axes of the slice: x: 4, y: 4 (y_hi: 2, y_lo: 2; y = y_hi * 2 + y_lo), z: 4, core: 2. Of those that a mesh axis runs over, the one named last changes fastest.
Arguments:
- inputs: bfloat16 [2, 8, 512, 1024], P(None, 'dp', 'tensor'), may hold values from -6 to 6
- segments: int32 [2, 8, 512], P(None, 'dp'), may hold values from 0 to 7, as said below
- qkv_weight: bfloat16 [2, 3, 1024, 1024], P('section', None, None, 'tensor'), may hold values from -0.1875 to 0.1875
- qv_bias: bfloat16 [2, 2, 1024], P('section', None, 'tensor'), may hold values from -3 to 3
- out_weight: bfloat16 [2, 1024, 1024], P('section', 'tensor'), may hold values from -0.5 to 0.5
- out_bias: bfloat16 [2, 1024], P('section'), may hold values from -3 to 3
- gain_one: bfloat16 [2, 1024], P('section'), may hold values from 0.5 to 1.5
- shift_one: bfloat16 [2, 1024], P('section'), may hold values from -3 to 3
- up_weight: bfloat16 [2, 1024, 4096], P('section', None, 'tensor'), may hold values from -0.1875 to 0.1875
- up_bias: bfloat16 [2, 4096], P('section', 'tensor'), may hold values from -3 to 3
- down_weight: bfloat16 [2, 4096, 1024], P('section', 'tensor'), may hold values from -0.09375 to 0.09375
- down_bias: bfloat16 [2, 1024], P('section'), may hold values from -3 to 3
- gain_two: bfloat16 [2, 1024], P('section'), may hold values from 0.5 to 1.5
- shift_two: bfloat16 [2, 1024], P('section'), may hold values from -3 to 3
- cotangent: bfloat16 [2, 8, 512, 1024], P(None, 'dp', 'tensor'), may hold values from -6 to 6
Outputs:
- layer_outputs: bfloat16 [2, 2, 8, 512, 1024], P('section', None, 'dp', 'tensor')
- input_grads: bfloat16 [2, 2, 8, 512, 1024], P('section', None, 'dp', 'tensor')
- grad_qkv: float32 [2, 3, 1024, 1024], P('section', None, None, 'tensor')
- grad_qv_bias: float32 [2, 2, 1024], P('section', None, 'tensor')
- grad_out_weight: float32 [2, 1024, 1024], P('section', 'tensor')
- grad_out_bias: float32 [2, 1024], P('section')
- grad_gain_one: float32 [2, 1024], P('section')
- grad_shift_one: float32 [2, 1024], P('section')
- grad_up_weight: float32 [2, 1024, 4096], P('section', None, 'tensor')
- grad_up_bias: float32 [2, 4096], P('section', 'tensor')
- grad_down_weight: float32 [2, 4096, 1024], P('section', 'tensor')
- grad_down_bias: float32 [2, 1024], P('section')
- grad_gain_two: float32 [2, 1024], P('section')
- grad_shift_two: float32 [2, 1024], P('section')
Inputs may be any that keep to these rules, and one draw needn't show every extreme that they name: `segments`: in every pack the numbers start at 0 at the first position and never fall, so each document is one run of positions; a position attends only to positions of its own document in its own pack.
All inputs are finite; a program needn't handle non-finite values.
Results may differ from a plain program's by a relative error of at most 0.028.
Values may be sent and summed in bfloat16 or wider, within the bound.
A program may use at most 128 MiB of HBM per device.

v0:
```python
import jax
import jax.numpy as jnp
from jax import lax
from jax.sharding import PartitionSpec as P

HEAD_DIM = 64


def from_behind(block, axis, distance):
    devices = range(lax.axis_size(axis))
    route = [(i - distance, i) for i in devices if i - distance in devices]
    return lax.ppermute(block, axis, route)


def layer_norm(values, gain, shift):
    center = values - jnp.mean(values, axis=-1, keepdims=True)
    spread = jnp.mean(center * center, axis=-1, keepdims=True)
    return center * lax.rsqrt(spread + 1e-06) * gain + shift


def gelu_exact(values):
    return jax.nn.gelu(values, approximate=False)


def contract_rows(left, right):
    return lax.dot_general(
        left, right, (((0,), (0,)), ((), ())), preferred_element_type=jnp.float32
    )


def contract_cols(left, right):
    return lax.dot_general(
        left, right, (((1,), (1,)), ((), ())), preferred_element_type=jnp.float32
    )


def masked_scores(queries, key_rows, seg_ids):
    scores = (
        jnp.einsum("pqhd,pkhd->phqk", queries, key_rows, preferred_element_type=jnp.float32) * 0.125
    )
    same_doc = (seg_ids[:, :, None] == seg_ids[:, None, :])[:, None]
    return jnp.where(same_doc, scores, -1e30)


def attend_forward(queries, key_rows, value_rows, seg_ids):
    scores = masked_scores(queries, key_rows, seg_ids)
    top_score = jnp.max(scores, axis=-1, keepdims=True)
    total = jnp.sum(jnp.exp(scores - top_score), axis=-1, keepdims=True)
    lse_rows = top_score + jnp.log(total)
    probs = jnp.exp(scores - lse_rows).astype(jnp.bfloat16)
    attended = jnp.einsum("phqk,pkhd->pqhd", probs, value_rows, preferred_element_type=jnp.float32)
    return (attended.astype(jnp.bfloat16), lse_rows)


def attend_backward(queries, key_rows, value_rows, seg_ids, lse_rows, grad_att):
    probs = jnp.exp(masked_scores(queries, key_rows, seg_ids) - lse_rows)
    grad_values = jnp.einsum(
        "phqk,pqhd->pkhd", probs.astype(jnp.bfloat16), grad_att, preferred_element_type=jnp.float32
    )
    grad_probs = jnp.einsum(
        "pqhd,pkhd->phqk", grad_att, value_rows, preferred_element_type=jnp.float32
    )
    grad_scores = probs * (grad_probs - jnp.sum(probs * grad_probs, axis=-1, keepdims=True))
    grad_scores = grad_scores.astype(jnp.bfloat16)
    grad_queries = (
        jnp.einsum("phqk,pkhd->pqhd", grad_scores, key_rows, preferred_element_type=jnp.float32)
        * 0.125
    )
    grad_keys = (
        jnp.einsum("phqk,pqhd->pkhd", grad_scores, queries, preferred_element_type=jnp.float32)
        * 0.125
    )
    return (grad_queries, grad_keys, grad_values)


def layer_forward(layer_in, seg_ids, params):
    qkv_w, qv_b, out_w, out_b, gain_a, shift_a, up_w, up_b, down_w, down_b, gain_b, shift_b = params
    pack_count = layer_in.shape[0]
    model_width = layer_in.shape[2]
    gathered = lax.all_gather(layer_in, "tensor", axis=1, tiled=True)
    seq_len = gathered.shape[1]
    token_rows = gathered.reshape(-1, model_width)
    projected = jnp.einsum("td,jdc->jtc", token_rows, qkv_w, preferred_element_type=jnp.float32)
    local_width = qkv_w.shape[2]
    head_shape = (pack_count, seq_len, local_width // HEAD_DIM, HEAD_DIM)
    queries = (projected[0] + qv_b[0]).astype(jnp.bfloat16).reshape(head_shape)
    key_rows = projected[1].astype(jnp.bfloat16).reshape(head_shape)
    value_rows = (projected[2] + qv_b[1]).astype(jnp.bfloat16).reshape(head_shape)
    attended, lse_rows = attend_forward(queries, key_rows, value_rows, seg_ids)
    att_keep = attended.reshape(-1, local_width)
    partial_value = jnp.dot(att_keep, out_w, preferred_element_type=jnp.float32).reshape(
        pack_count, seq_len, model_width
    )
    projected_out = lax.psum_scatter(
        partial_value.astype(jnp.bfloat16), "tensor", scatter_dimension=1, tiled=True
    ).astype(jnp.float32)
    residual = layer_in.astype(jnp.float32) + projected_out + out_b
    normed = layer_norm(residual, gain_a, shift_a)
    normed_all = lax.all_gather(normed.astype(jnp.bfloat16), "tensor", axis=1, tiled=True).reshape(
        -1, model_width
    )
    hidden = jnp.dot(normed_all, up_w, preferred_element_type=jnp.float32) + up_b
    active = gelu_exact(hidden).astype(jnp.bfloat16)
    partial_two = jnp.dot(active, down_w, preferred_element_type=jnp.float32).reshape(
        pack_count, seq_len, model_width
    )
    second = (
        normed
        + lax.psum_scatter(
            partial_two.astype(jnp.bfloat16), "tensor", scatter_dimension=1, tiled=True
        ).astype(jnp.float32)
        + down_b
    )
    output = layer_norm(second, gain_b, shift_b)
    saved_state = (
        token_rows,
        queries,
        key_rows,
        value_rows,
        lse_rows,
        att_keep,
        residual,
        normed_all,
        hidden,
        active,
        second,
        seg_ids,
    )
    return (output, saved_state)


def mlp_backward(saved_state, grad_out, params):
    qkv_w, qv_b, out_w, out_b, gain_a, shift_a, up_w, up_b, down_w, down_b, gain_b, shift_b = params
    (
        token_rows,
        queries,
        key_rows,
        value_rows,
        lse_rows,
        att_keep,
        residual,
        normed_all,
        hidden,
        active,
        second,
        seg_ids,
    ) = saved_state
    pack_count = second.shape[0]
    model_width = second.shape[2]
    unused_out, norm_back = jax.vjp(layer_norm, second, gain_b, shift_b)
    grad_second, grad_gain_b, grad_shift_b = norm_back(grad_out)
    grad_down_b = jnp.sum(grad_second, axis=(0, 1))
    grad_mlp = lax.all_gather(
        grad_second.astype(jnp.bfloat16), "tensor", axis=1, tiled=True
    ).reshape(-1, model_width)
    grad_down_w = contract_rows(active, grad_mlp)
    grad_active = contract_cols(grad_mlp, down_w)
    unused_gelu, gelu_back = jax.vjp(gelu_exact, hidden)
    grad_hidden = gelu_back(grad_active)[0]
    grad_up_b = jnp.sum(grad_hidden, axis=0)
    grad_hidden_low = grad_hidden.astype(jnp.bfloat16)
    grad_up_w = contract_rows(normed_all, grad_hidden_low)
    partial_value = contract_cols(grad_hidden_low, up_w).reshape(pack_count, -1, model_width)
    grad_normed = grad_second + lax.psum_scatter(
        partial_value.astype(jnp.bfloat16), "tensor", scatter_dimension=1, tiled=True
    ).astype(jnp.float32)
    return (
        grad_normed,
        (grad_up_w, grad_up_b, grad_down_w),
        (grad_down_b, grad_gain_b, grad_shift_b),
    )


def attn_backward(saved_state, grad_normed, params):
    qkv_w, qv_b, out_w, out_b, gain_a, shift_a, up_w, up_b, down_w, down_b, gain_b, shift_b = params
    (
        token_rows,
        queries,
        key_rows,
        value_rows,
        lse_rows,
        att_keep,
        residual,
        normed_all,
        hidden,
        active,
        second,
        seg_ids,
    ) = saved_state
    pack_count = residual.shape[0]
    model_width = residual.shape[2]
    local_width = qkv_w.shape[2]
    unused_out, norm_back = jax.vjp(layer_norm, residual, gain_a, shift_a)
    grad_residual, grad_gain_a, grad_shift_a = norm_back(grad_normed)
    grad_out_b = jnp.sum(grad_residual, axis=(0, 1))
    grad_low = grad_residual.astype(jnp.bfloat16)
    grad_proj = lax.all_gather(grad_low, "tensor", axis=1, tiled=True).reshape(-1, model_width)
    grad_out_w = contract_rows(att_keep, grad_proj)
    grad_att = contract_cols(grad_proj, out_w).astype(jnp.bfloat16).reshape(queries.shape)
    grad_queries, grad_keys, grad_values = attend_backward(
        queries, key_rows, value_rows, seg_ids, lse_rows, grad_att
    )
    grad_qkv_rows = (
        jnp.stack([grad_queries, grad_keys, grad_values])
        .astype(jnp.bfloat16)
        .reshape(3, -1, local_width)
    )
    grad_qv_b = jnp.stack(
        [
            jnp.sum(grad_qkv_rows[0].astype(jnp.float32), axis=0),
            jnp.sum(grad_qkv_rows[2].astype(jnp.float32), axis=0),
        ]
    )
    grad_qkv_w = jnp.einsum(
        "td,jtc->jdc", token_rows, grad_qkv_rows, preferred_element_type=jnp.float32
    )
    partial_value = jnp.einsum(
        "jtc,jdc->td", grad_qkv_rows, qkv_w, preferred_element_type=jnp.float32
    ).reshape(pack_count, -1, model_width)
    grad_input = grad_residual + lax.psum_scatter(
        partial_value.astype(jnp.bfloat16), "tensor", scatter_dimension=1, tiled=True
    ).astype(jnp.float32)
    return (
        grad_input,
        (grad_qkv_w, grad_qv_b, grad_out_w),
        (grad_out_b, grad_gain_a, grad_shift_a),
    )


def add_masked(totals, terms, is_valid):
    if totals is None:
        return tuple((jnp.where(is_valid, term, 0.0) for term in terms))
    return tuple((total + jnp.where(is_valid, term, 0.0) for total, term in zip(totals, terms)))


def local(
    inputs,
    segments,
    qkv_weight,
    qv_bias,
    out_weight,
    out_bias,
    gain_one,
    shift_one,
    up_weight,
    up_bias,
    down_weight,
    down_bias,
    gain_two,
    shift_two,
    cotangent,
):
    section_index = lax.axis_index("section")
    section_count = lax.axis_size("section")
    micro_count = inputs.shape[0]
    step_count = micro_count + section_count - 1
    is_first = section_index == 0
    is_last = section_index == section_count - 1
    params = (
        qkv_weight[0],
        qv_bias[0].astype(jnp.float32),
        out_weight[0],
        out_bias[0].astype(jnp.float32),
        gain_one[0].astype(jnp.float32),
        shift_one[0].astype(jnp.float32),
        up_weight[0],
        up_bias[0].astype(jnp.float32),
        down_weight[0],
        down_bias[0].astype(jnp.float32),
        gain_two[0].astype(jnp.float32),
        shift_two[0].astype(jnp.float32),
    )
    received = jnp.zeros_like(inputs[0])
    outputs_list = []
    saved_list = []
    for moment in range(step_count):
        micro_index = jnp.clip(moment - section_index, 0, micro_count - 1)
        seg_ids = lax.dynamic_index_in_dim(segments, micro_index, 0, keepdims=False)
        layer_in = jnp.where(is_first, inputs[min(moment, micro_count - 1)], received)
        output, saved_state = layer_forward(layer_in, seg_ids, params)
        outputs_list.append(output)
        saved_list.append(saved_state)
        if moment + 1 < step_count:
            received = from_behind(output.astype(jnp.bfloat16), "section", 1)
    stacked_out = jnp.stack(outputs_list)
    layer_outputs = lax.dynamic_slice_in_dim(stacked_out, section_index, micro_count, 0).astype(
        jnp.bfloat16
    )[None]
    saved_stack = jax.tree.map(lambda *leaves: jnp.stack(leaves), *saved_list)
    received_grad = jnp.zeros(inputs[0].shape, jnp.float32)
    mlp_totals = None
    attn_totals = None
    small_mlp = None
    small_attn = None
    grads_list = []
    for moment in range(step_count):
        micro_index = moment - (section_count - 1 - section_index)
        is_valid = (micro_index >= 0) & (micro_index < micro_count)
        kept_index = jnp.clip(micro_index + section_index, 0, step_count - 1)
        state_now = jax.tree.map(
            lambda leaf: lax.dynamic_index_in_dim(leaf, kept_index, 0, keepdims=False), saved_stack
        )
        grad_out = jnp.where(
            is_last, cotangent[min(moment, micro_count - 1)].astype(jnp.float32), received_grad
        )
        grad_normed, mlp_terms, small_terms = mlp_backward(state_now, grad_out, params)
        mlp_totals = add_masked(mlp_totals, mlp_terms, is_valid)
        small_mlp = add_masked(small_mlp, small_terms, is_valid)
        grad_input, attn_terms, small_terms_a = attn_backward(state_now, grad_normed, params)
        attn_totals = add_masked(attn_totals, attn_terms, is_valid)
        small_attn = add_masked(small_attn, small_terms_a, is_valid)
        grads_list.append(grad_input)
        if moment + 1 < step_count:
            received_grad = from_behind(grad_input.astype(jnp.bfloat16), "section", -1).astype(
                jnp.float32
            )
    stacked_grads = jnp.stack(grads_list)
    input_grads = lax.dynamic_slice_in_dim(
        stacked_grads, section_count - 1 - section_index, micro_count, 0
    ).astype(jnp.bfloat16)[None]
    summed = (
        lax.psum(attn_totals[0].astype(jnp.bfloat16), "dp").astype(jnp.float32),
        lax.psum(attn_totals[1].astype(jnp.bfloat16), "dp").astype(jnp.float32),
        lax.psum(attn_totals[2].astype(jnp.bfloat16), "dp").astype(jnp.float32),
        lax.psum(mlp_totals[0].astype(jnp.bfloat16), "dp").astype(jnp.float32),
        lax.psum(mlp_totals[1].astype(jnp.bfloat16), "dp").astype(jnp.float32),
        lax.psum(mlp_totals[2].astype(jnp.bfloat16), "dp").astype(jnp.float32),
    )
    attn_totals = (summed[0], summed[1], summed[2])
    mlp_totals = (summed[3], summed[4], summed[5])
    small_sums = lax.psum(
        (small_attn[0], small_attn[1], small_attn[2], small_mlp[0], small_mlp[1], small_mlp[2]),
        ("tensor", "dp"),
    )
    return (
        layer_outputs,
        input_grads,
        attn_totals[0][None],
        attn_totals[1][None],
        attn_totals[2][None],
        small_sums[0][None],
        small_sums[1][None],
        small_sums[2][None],
        mlp_totals[0][None],
        mlp_totals[1][None],
        mlp_totals[2][None],
        small_sums[3][None],
        small_sums[4][None],
        small_sums[5][None],
    )


def solution(mesh):
    return jax.shard_map(
        local,
        mesh=mesh,
        in_specs=(
            P(None, "dp", "tensor", None),
            P(None, "dp", None),
            P("section", None, None, "tensor"),
            P("section", None, "tensor"),
            P("section", "tensor", None),
            P("section", None),
            P("section", None),
            P("section", None),
            P("section", None, "tensor"),
            P("section", "tensor"),
            P("section", "tensor", None),
            P("section", None),
            P("section", None),
            P("section", None),
            P(None, "dp", "tensor", None),
        ),
        out_specs=(
            P("section", None, "dp", "tensor", None),
            P("section", None, "dp", "tensor", None),
            P("section", None, None, "tensor"),
            P("section", None, "tensor"),
            P("section", "tensor", None),
            P("section", None),
            P("section", None),
            P("section", None),
            P("section", None, "tensor"),
            P("section", "tensor"),
            P("section", "tensor", None),
            P("section", None),
            P("section", None),
            P("section", None),
        ),
        check_vma=False,
    )
```

profile of v0, /device:TPU:1, one launch (start us, length us, event | category | flops | bytes accessed | tf_op | source)
XLA Modules:
  0.0 1908.0 jit_solution(7199502427455003315)
XLA Ops:
  12.8 47.8 %all-gather.36.cloned.1.call-done = bf16[1,1,512,1024]{3,2,1,0:T(8,128)(2,1)} async-done(((bf16[1,1,64,1024]{3,2,1,0:T(8,128)(2,1)}), bf16[1,1,512,1024]{3,2,1,0:T(8,128)(2,1)}) %all-gather.36.cloned.1.call-update) | async-done | bytes 1048592 | tf_op jit(solution)/shard_map/all_gather | solution.py:80
  65.7 69.9 %reduce-scatter.13.cloned.1.call-done = bf16[1,64,1024]{2,1,0:T(8,128)(2,1)} async-done(((bf16[1,512,1024]{2,1,0:T(8,128)(2,1)}), bf16[1,64,1024]{2,1,0:T(8,128)(2,1)}) %reduce-scatter.13.cloned.1.call-update) | async-done | bytes 131088 | tf_op jit(solution)/shard_map/reduce_scatter | solution.py:94
  140.3 47.4 %all-gather.14.cloned.1.call-done = bf16[1,512,1024]{2,1,0:T(8,128)(2,1)} async-done(((bf16[1,64,1024]{2,1,0:T(8,128)(2,1)}), bf16[1,512,1024]{2,1,0:T(8,128)(2,1)}) %all-gather.14.cloned.1.call-update) | async-done | bytes 1048592 | tf_op jit(solution)/shard_map/all_gather | solution.py:99
  187.7 5.0 fusion.27
  194.6 69.9 %reduce-scatter.15.cloned.1.call-done = bf16[1,64,1024]{2,1,0:T(8,128)(2,1)} async-done(((bf16[1,512,1024]{2,1,0:T(8,128)(2,1)}), bf16[1,64,1024]{2,1,0:T(8,128)(2,1)}) %reduce-scatter.15.cloned.1.call-update) | async-done | bytes 131088 | tf_op jit(solution)/shard_map/reduce_scatter | solution.py:109
  271.4 49.3 %all-gather.16.cloned.1.call-done = bf16[1,512,1024]{2,1,0:T(8,128)(2,1)} async-done(((bf16[1,64,1024]{2,1,0:T(8,128)(2,1)}), bf16[1,512,1024]{2,1,0:T(8,128)(2,1)}) %all-gather.16.cloned.1.call-update) | async-done | bytes 1048592 | tf_op jit(solution)/shard_map/all_gather | solution.py:80
  325.7 70.0 %reduce-scatter.17.cloned.1.call-done = bf16[1,64,1024]{2,1,0:T(8,128)(2,1)} async-done(((bf16[1,512,1024]{2,1,0:T(8,128)(2,1)}), bf16[1,64,1024]{2,1,0:T(8,128)(2,1)}) %reduce-scatter.17.cloned.1.call-update) | async-done | bytes 131088 | tf_op jit(solution)/shard_map/reduce_scatter | solution.py:94
  399.7 47.4 %all-gather.18.cloned.1.call-done = bf16[1,512,1024]{2,1,0:T(8,128)(2,1)} async-done(((bf16[1,64,1024]{2,1,0:T(8,128)(2,1)}), bf16[1,512,1024]{2,1,0:T(8,128)(2,1)}) %all-gather.18.cloned.1.call-update) | async-done | bytes 1048592 | tf_op jit(solution)/shard_map/all_gather | solution.py:99
  447.1 5.0 fusion.30
  454.7 70.0 %reduce-scatter.19.cloned.1.call-done = bf16[1,64,1024]{2,1,0:T(8,128)(2,1)} async-done(((bf16[1,512,1024]{2,1,0:T(8,128)(2,1)}), bf16[1,64,1024]{2,1,0:T(8,128)(2,1)}) %reduce-scatter.19.cloned.1.call-update) | async-done | bytes 131088 | tf_op jit(solution)/shard_map/reduce_scatter | solution.py:109
  534.5 48.1 %all-gather.20.cloned.1.call-done = bf16[1,512,1024]{2,1,0:T(8,128)(2,1)} async-done(((bf16[1,64,1024]{2,1,0:T(8,128)(2,1)}), bf16[1,512,1024]{2,1,0:T(8,128)(2,1)}) %all-gather.20.cloned.1.call-update) | async-done | bytes 1048592 | tf_op jit(solution)/shard_map/all_gather | solution.py:80
  588.2 70.0 %reduce-scatter.21.cloned.1.call-done = bf16[1,64,1024]{2,1,0:T(8,128)(2,1)} async-done(((bf16[1,512,1024]{2,1,0:T(8,128)(2,1)}), bf16[1,64,1024]{2,1,0:T(8,128)(2,1)}) %reduce-scatter.21.cloned.1.call-update) | async-done | bytes 131088 | tf_op jit(solution)/shard_map/reduce_scatter | solution.py:94
  662.8 47.4 %all-gather.22.cloned.1.call-done = bf16[1,512,1024]{2,1,0:T(8,128)(2,1)} async-done(((bf16[1,64,1024]{2,1,0:T(8,128)(2,1)}), bf16[1,512,1024]{2,1,0:T(8,128)(2,1)}) %all-gather.22.cloned.1.call-update) | async-done | bytes 1048592 | tf_op jit(solution)/shard_map/all_gather | solution.py:99
  710.2 5.0 fusion.33
  718.9 69.0 %reduce-scatter.23.cloned.1.call-done = bf16[1,64,1024]{2,1,0:T(8,128)(2,1)} async-done(((bf16[1,512,1024]{2,1,0:T(8,128)(2,1)}), bf16[1,64,1024]{2,1,0:T(8,128)(2,1)}) %reduce-scatter.23.cloned.1.call-update) | async-done | bytes 131088 | tf_op jit(solution)/shard_map/reduce_scatter | solution.py:109
  798.0 43.4 %all-gather.24.cloned.1.call-done = bf16[1,512,1024]{2,1,0:T(8,128)(2,1)} async-done(((bf16[1,64,1024]{2,1,0:T(8,128)(2,1)}), bf16[1,512,1024]{2,1,0:T(8,128)(2,1)}) %all-gather.24.cloned.1.call-update) | async-done | bytes 1048592 | tf_op jit(solution)/shard_map/all_gather | solution.py:153
  841.5 5.4 fusion.349
  854.3 65.2 %reduce-scatter.25.cloned.1.call-done = bf16[1,64,1024]{2,1,0:T(8,128)(2,1)} async-done(((bf16[1,512,1024]{2,1,0:T(8,128)(2,1)}), bf16[1,64,1024]{2,1,0:T(8,128)(2,1)}) %reduce-scatter.25.cloned.1.call-update) | async-done | bytes 131088 | tf_op jit(solution)/shard_map/reduce_scatter | solution.py:164
  932.5 40.5 %all-gather.26.cloned.1.call-done = bf16[1,512,1024]{2,1,0:T(8,128)(2,1)} async-done(((bf16[1,64,1024]{2,1,0:T(8,128)(2,1)}), bf16[1,512,1024]{2,1,0:T(8,128)(2,1)}) %all-gather.26.cloned.1.call-update) | async-done | bytes 1048592 | tf_op jit(solution)/shard_map/all_gather | solution.py:197
  989.5 70.0 %reduce-scatter.27.cloned.1.call-done = bf16[1,64,1024]{2,1,0:T(8,128)(2,1)} async-done(((bf16[1,512,1024]{2,1,0:T(8,128)(2,1)}), bf16[1,64,1024]{2,1,0:T(8,128)(2,1)}) %reduce-scatter.27.cloned.1.call-update) | async-done | bytes 131088 | tf_op jit(solution)/shard_map/reduce_scatter | solution.py:220
  1061.9 4.4 collective-permute-done.2
  1071.2 48.6 %all-gather.28.cloned.1.call-done = bf16[1,512,1024]{2,1,0:T(8,128)(2,1)} async-done(((bf16[1,64,1024]{2,1,0:T(8,128)(2,1)}), bf16[1,512,1024]{2,1,0:T(8,128)(2,1)}) %all-gather.28.cloned.1.call-update) | async-done | bytes 1048592 | tf_op jit(solution)/shard_map/all_gather | solution.py:153
  1119.8 5.4 fusion.348
  1127.8 70.0 %reduce-scatter.29.cloned.1.call-done = bf16[1,64,1024]{2,1,0:T(8,128)(2,1)} async-done(((bf16[1,512,1024]{2,1,0:T(8,128)(2,1)}), bf16[1,64,1024]{2,1,0:T(8,128)(2,1)}) %reduce-scatter.29.cloned.1.call-update) | async-done | bytes 131088 | tf_op jit(solution)/shard_map/reduce_scatter | solution.py:164
  1204.2 46.2 %all-gather.30.cloned.1.call-done = bf16[1,512,1024]{2,1,0:T(8,128)(2,1)} async-done(((bf16[1,64,1024]{2,1,0:T(8,128)(2,1)}), bf16[1,512,1024]{2,1,0:T(8,128)(2,1)}) %all-gather.30.cloned.1.call-update) | async-done | bytes 1048592 | tf_op jit(solution)/shard_map/all_gather | solution.py:197
  1266.9 70.0 %reduce-scatter.31.cloned.1.call-done = bf16[1,64,1024]{2,1,0:T(8,128)(2,1)} async-done(((bf16[1,512,1024]{2,1,0:T(8,128)(2,1)}), bf16[1,64,1024]{2,1,0:T(8,128)(2,1)}) %reduce-scatter.31.cloned.1.call-update) | async-done | bytes 131088 | tf_op jit(solution)/shard_map/reduce_scatter | solution.py:220
  1348.7 48.5 %all-gather.32.cloned.1.call-done = bf16[1,512,1024]{2,1,0:T(8,128)(2,1)} async-done(((bf16[1,64,1024]{2,1,0:T(8,128)(2,1)}), bf16[1,512,1024]{2,1,0:T(8,128)(2,1)}) %all-gather.32.cloned.1.call-update) | async-done | bytes 1048592 | tf_op jit(solution)/shard_map/all_gather | solution.py:153
  1397.3 5.4 fusion.347
  1419.4 55.1 %reduce-scatter.33.cloned.1.call-done = bf16[1,64,1024]{2,1,0:T(8,128)(2,1)} async-done(((bf16[1,512,1024]{2,1,0:T(8,128)(2,1)}), bf16[1,64,1024]{2,1,0:T(8,128)(2,1)}) %reduce-scatter.33.cloned.1.call-update) | async-done | bytes 131088 | tf_op jit(solution)/shard_map/reduce_scatter | solution.py:164
  1493.1 33.9 %all-gather.34.cloned.1.call-done = bf16[1,512,1024]{2,1,0:T(8,128)(2,1)} async-done(((bf16[1,64,1024]{2,1,0:T(8,128)(2,1)}), bf16[1,512,1024]{2,1,0:T(8,128)(2,1)}) %all-gather.34.cloned.1.call-update) | async-done | bytes 1048592 | tf_op jit(solution)/shard_map/all_gather | solution.py:197
  1551.6 319.8 %all-reduce = (f32[1,1024]{1,0:T(1,128)}, f32[1,1024]{1,0:T(1,128)}, f32[1,1024]{1,0:T(1,128)}, f32[1,1024]{1,0:T(1,128)}, f32[1,1024]{1,0:T(1,128)}, /*index=5*/f32[1,1024]{1,0:T(1,128)}) all-reduce(f32[1,1024]{1,0:T(1,128)S(1)} %bitcast.904, ...), channel_id=1, replica_groups=mesh['section'=2,'tensor'=8,'dp'=8] {'tensor','dp'}, use_global_device_ids=true, to_apply=%region_69.70 | all-reduce | flops 6144 | bytes 49152 | tf_op jit(solution)/shard_map/psum | solution.py:331
  1871.5 19.8 %all-reduce.1 = (bf16[1,2,128]{2,1,0:T(2,128)(2,1)S(1)}, bf16[1,512]{1,0:T(2,128)(2,1)S(1)}) all-reduce(bf16[1,2,128]{2,1,0:T(2,128)(2,1)S(1)} %fusion.313, bf16[1,512]{1,0:T(2,128)(2,1)S(1)} %broadcast_in_dim.331), channel_id=1, replica_groups=mesh['section'=2,'tensor'=8,'dp'=8] {'dp'}, use_global_device_ids=true, to_apply=%region_64.65 | all-reduce | flops 768 | bytes 3072 | tf_op jit(solution)/shard_map/psum | solution.py:323
  (639 shorter events, 218.2 us)
Async XLA Ops:
  7.2 53.4 %all-gather.36.cloned.1.call-start = ((), (), s32[]{:S(2)}) async-start(), calls=%async_computation.35 | async-start | bytes 1179648 | tf_op jit(solution)/shard_map/all_gather | solution.py:80
  8.9 126.7 %reduce-scatter.13.cloned.1.call-start = ((), (), s32[]{:S(2)}) async-start(), calls=%async_computation.12 | async-start | bytes 1179648 | tf_op jit(solution)/shard_map/reduce_scatter | solution.py:94
  11.2 312.5 %copy-start.127 = (f32[2,64]{1,0:T(2,128)}, f32[2,64]{1,0:T(2,128)S(1)}, u32[]{:S(2)}) copy-start(f32[2,64]{1,0:T(2,128)S(1)} %add.609) | copy-start | bytes 1540
  65.6 122.0 %all-gather.14.cloned.1.call-start = ((), (), s32[]{:S(2)}) async-start(), calls=%async_computation.13 | async-start | bytes 1179648 | tf_op jit(solution)/shard_map/all_gather | solution.py:99
  140.2 124.3 %reduce-scatter.15.cloned.1.call-start = ((), (), s32[]{:S(2)}) async-start(), calls=%async_computation.14 | async-start | bytes 1179648 | tf_op jit(solution)/shard_map/reduce_scatter | solution.py:109
  194.4 126.3 %all-gather.16.cloned.1.call-start = ((), (), s32[]{:S(2)}) async-start(), calls=%async_computation.15 | async-start | bytes 1179648 | tf_op jit(solution)/shard_map/all_gather | solution.py:80
  266.0 4.5 collective-permute-start
  271.1 124.6 %reduce-scatter.17.cloned.1.call-start = ((), (), s32[]{:S(2)}) async-start(), calls=%async_computation.16 | async-start | bytes 1179648 | tf_op jit(solution)/shard_map/reduce_scatter | solution.py:94
  325.7 121.4 %all-gather.18.cloned.1.call-start = ((), (), s32[]{:S(2)}) async-start(), calls=%async_computation.17 | async-start | bytes 1179648 | tf_op jit(solution)/shard_map/all_gather | solution.py:99
  399.7 125.1 %reduce-scatter.19.cloned.1.call-start = ((), (), s32[]{:S(2)}) async-start(), calls=%async_computation.18 | async-start | bytes 1179648 | tf_op jit(solution)/shard_map/reduce_scatter | solution.py:109
  454.6 127.9 %all-gather.20.cloned.1.call-start = ((), (), s32[]{:S(2)}) async-start(), calls=%async_computation.19 | async-start | bytes 1179648 | tf_op jit(solution)/shard_map/all_gather | solution.py:80
  527.8 4.5 collective-permute-start.1
  533.0 125.2 %reduce-scatter.21.cloned.1.call-start = ((), (), s32[]{:S(2)}) async-start(), calls=%async_computation.20 | async-start | bytes 1179648 | tf_op jit(solution)/shard_map/reduce_scatter | solution.py:94
  588.1 122.1 %all-gather.22.cloned.1.call-start = ((), (), s32[]{:S(2)}) async-start(), calls=%async_computation.21 | async-start | bytes 1179648 | tf_op jit(solution)/shard_map/all_gather | solution.py:99
  662.7 125.1 %reduce-scatter.23.cloned.1.call-start = ((), (), s32[]{:S(2)}) async-start(), calls=%async_computation.22 | async-start | bytes 1179648 | tf_op jit(solution)/shard_map/reduce_scatter | solution.py:109
  717.8 123.7 %all-gather.24.cloned.1.call-start = ((), (), s32[]{:S(2)}) async-start(), calls=%async_computation.23 | async-start | bytes 1179648 | tf_op jit(solution)/shard_map/all_gather | solution.py:153
  794.0 125.5 %reduce-scatter.25.cloned.1.call-start = ((), (), s32[]{:S(2)}) async-start(), calls=%async_computation.24 | async-start | bytes 1179648 | tf_op jit(solution)/shard_map/reduce_scatter | solution.py:164
  849.5 123.5 %all-gather.26.cloned.1.call-start = ((), (), s32[]{:S(2)}) async-start(), calls=%async_computation.25 | async-start | bytes 1179648 | tf_op jit(solution)/shard_map/all_gather | solution.py:197
  925.5 134.0 %reduce-scatter.27.cloned.1.call-start = ((), (), s32[]{:S(2)}) async-start(), calls=%async_computation.26 | async-start | bytes 1179648 | tf_op jit(solution)/shard_map/reduce_scatter | solution.py:220
  989.4 130.3 %all-gather.28.cloned.1.call-start = ((), (), s32[]{:S(2)}) async-start(), calls=%async_computation.27 | async-start | bytes 1179648 | tf_op jit(solution)/shard_map/all_gather | solution.py:153
  1060.6 5.7 collective-permute-start.2
  1071.2 126.6 %reduce-scatter.29.cloned.1.call-start = ((), (), s32[]{:S(2)}) async-start(), calls=%async_computation.28 | async-start | bytes 1179648 | tf_op jit(solution)/shard_map/reduce_scatter | solution.py:164
  1127.8 122.7 %all-gather.30.cloned.1.call-start = ((), (), s32[]{:S(2)}) async-start(), calls=%async_computation.29 | async-start | bytes 1179648 | tf_op jit(solution)/shard_map/all_gather | solution.py:197
  1203.0 133.9 %reduce-scatter.31.cloned.1.call-start = ((), (), s32[]{:S(2)}) async-start(), calls=%async_computation.30 | async-start | bytes 1179648 | tf_op jit(solution)/shard_map/reduce_scatter | solution.py:220
  1266.9 130.4 %all-gather.32.cloned.1.call-start = ((), (), s32[]{:S(2)}) async-start(), calls=%async_computation.31 | async-start | bytes 1179648 | tf_op jit(solution)/shard_map/all_gather | solution.py:153
  1338.1 5.7 collective-permute-start.3
  1348.7 125.9 %reduce-scatter.33.cloned.1.call-start = ((), (), s32[]{:S(2)}) async-start(), calls=%async_computation.32 | async-start | bytes 1179648 | tf_op jit(solution)/shard_map/reduce_scatter | solution.py:164
  1404.5 122.5 %all-gather.34.cloned.1.call-start = ((), (), s32[]{:S(2)}) async-start(), calls=%async_computation.33 | async-start | bytes 1179648 | tf_op jit(solution)/shard_map/all_gather | solution.py:197
  1479.5 413.0 %all-reduce.5.cloned.1.call-start = ((), (), s32[]{:S(2)}) async-start(), calls=%async_computation.36 | async-start | bytes 6291456 | tf_op jit(solution)/shard_map/psum | solution.py:322
  1544.4 354.8 %reduce-scatter.35.cloned.1.call-start = ((), (), s32[]{:S(2)}) async-start(), calls=%async_computation.34 | async-start | bytes 1179648 | tf_op jit(solution)/shard_map/reduce_scatter | solution.py:220
  1549.1 322.3 %copy-start.168 = (f32[2,64]{1,0:T(2,128)S(1)}, f32[2,64]{1,0:T(2,128)}, u32[]{:S(2)}) copy-start(f32[2,64]{1,0:T(2,128)} %get-tuple-element.144) | copy-start | bytes 1540
  1549.1 322.3 %copy-start.170 = (f32[2,64]{1,0:T(2,128)S(1)}, f32[2,64]{1,0:T(2,128)}, u32[]{:S(2)}) copy-start(f32[2,64]{1,0:T(2,128)} %get-tuple-element.146) | copy-start | bytes 1540
  (178 other events, 3866.8 us)
Sparse Core Ops, SparseCore 0:
  10.9 49.5 all-gather.35
  65.7 69.8 reduce-scatter.12
  140.3 47.2 all-gather.13
  194.6 69.8 reduce-scatter.14
  271.3 49.4 all-gather.15
  325.8 69.9 reduce-scatter.16
  399.8 47.2 all-gather.17
  454.8 69.9 reduce-scatter.18
  533.1 49.4 all-gather.19
  588.2 69.8 reduce-scatter.20
  662.8 47.3 all-gather.21
  717.9 69.9 reduce-scatter.22
  794.1 47.2 all-gather.23
  849.6 69.9 reduce-scatter.24
  925.6 47.2 all-gather.25
  989.6 69.8 reduce-scatter.26
  1071.3 48.4 all-gather.27
  1127.9 69.8 reduce-scatter.28
  1203.1 47.2 all-gather.29
  1267.0 69.8 reduce-scatter.30
  1348.8 48.4 all-gather.31
  1404.6 69.8 reduce-scatter.32
  1479.6 47.2 all-gather.33
  1544.5 67.6 all-reduce.4
  1616.3 71.7 reduce-scatter.34
where the time goes:
time: 1920 us; the launch traced here: 1910 us
  waiting for transfers between devices  1310 us (68%)
  blocking collectives  340 us (18%)
  matrix products  113 us (6%)
  other arithmetic  81.1 us (4%)
  local copies, waits for them, and re-layouts  37.7 us (2%)
    psum x1, blocking collectives, local(): lax.psum((small_attn[0], small_attn[1], small_attn[2], small_mlp[0], smal...  320 us
    reduce_scatter x3, waiting for transfers between devices, layer_forward(): lax.psum_scatter(partial_value.astype(jnp.bfloat16), 'tensor', scatter_di...  210 us
    reduce_scatter x3, waiting for transfers between devices, layer_forward(): lax.psum_scatter(partial_two.astype(jnp.bfloat16), 'tensor', scatter_dime...  209 us
    reduce_scatter x3, waiting for transfers between devices, mlp_backward(): lax.psum_scatter(partial_value.astype(jnp.bfloat16), 'tensor', scatter_di...  190 us
    all_gather x3, waiting for transfers between devices, layer_forward(): gathered = lax.all_gather(layer_in, 'tensor', axis=1, tiled=True)  145 us
    all_gather x3, waiting for transfers between devices, layer_forward(): lax.all_gather(normed.astype(jnp.bfloat16), 'tensor', axis=1, tiled=True)  142 us
    all_gather x3, waiting for transfers between devices, mlp_backward(): lax.all_gather(grad_second.astype(jnp.bfloat16), 'tensor', axis=1, tiled=...  141 us
    reduce_scatter x3, waiting for transfers between devices, attn_backward(): lax.psum_scatter(partial_value.astype(jnp.bfloat16), 'tensor', scatter_di...  140 us
  transfers between devices with their start and end apart: 29, of which 27 were waited for; matrix products, arithmetic and copies ran while one was open for 3% of the time, Pallas kernels for 0%

commit v1 on v0

v1 whole, which is shorter than its diff:
```python
import jax
import jax.numpy as jnp
from jax import lax
from jax.experimental import pallas as pl
from jax.experimental.pallas import tpu as pltpu
from jax.sharding import Mesh
from jax.sharding import PartitionSpec as P


BF = jnp.bfloat16
F32 = jnp.float32
MESH = pl.DeviceIdType.MESH
D = 1024
FFS = 512
SEQ = 512
BLK = 64
QKV, OUT, UP, DOWN = 0, 1, 2, 3
PIECE = (256, 32, 256, 128)
FA, FM, BM, BA = 0, 1, 2, 3


def remote(src, dst, send, recv, dev):
    return pltpu.make_async_remote_copy(
        src_ref=src, dst_ref=dst, send_sem=send, recv_sem=recv, device_id=dev, device_id_type=MESH
    )


def dot_nn(a, b):
    return lax.dot_general(a, b, (((1,), (0,)), ((), ())), preferred_element_type=F32)


def dot_nt(a, b):
    return lax.dot_general(a, b, (((1,), (1,)), ((), ())), preferred_element_type=F32)


def dot_tn(a, b):
    return lax.dot_general(a, b, (((0,), (0,)), ((), ())), preferred_element_type=F32)


def normed(r):
    center = r - jnp.mean(r, axis=-1, keepdims=True)
    scale = lax.rsqrt(jnp.mean(center * center, axis=-1, keepdims=True) + 1e-06)
    return center * scale, scale


def norm_back(dy, gain, n, scale):
    e = dy * gain
    mean_e = jnp.mean(e, axis=-1, keepdims=True)
    mean_en = jnp.mean(e * n, axis=-1, keepdims=True)
    return (e - mean_e - n * mean_en) * scale


def col_sum(v):
    return jnp.sum(v, axis=0, keepdims=True)


def kernel(
    inp, cot, seg, wq_in, wo_in, wu_in, wd_in, sw_in,
    lo, ig, gq, go, gu, gd, gs,
    wq, wo, wu, wd, sw,
    hbuf, arbuf, dmbuf, dprbuf,
    ain, bin_, aout, bout, part,
    qkv, att, probs, gp, gr, n1, n2, sc1, sc2, abuf, res,
    segb, bias, cotb, dur, dacc, dx,
    yb, lob, dhb, igb, gsb,
    g0, g1, g2, g3,
    zr0, zr1, zr2, zr3,
    yo0, yo1, yo2, yo3,
    yr0, yr1, yr2, yr3,
    f0, f1, f2, f3,
    swap_s, swap_r, wy_s, wy_r, wz_s, wz_r, wl,
    ag_s, ag_r, cg_s, cg_r, ra_s, ra_r, rb_s, rb_r,
    lo_s, lo_r, ig_s, ig_r,
    gz_s, gz_r, gy_s, gy_r, fz_s, fz_r, fc_s, fc_r, st,
):
    s = lax.axis_index("s")
    x = lax.axis_index("x")
    yh = lax.axis_index("yh")
    z = lax.axis_index("z")
    c = lax.axis_index("c")
    diag = c == yh
    weights_in = (wq_in, wo_in, wu_in, wd_in)
    weights = (wq, wo, wu, wd)
    grads = (g0, g1, g2, g3)
    zrecv = (zr0, zr1, zr2, zr3)
    yout = (yo0, yo1, yo2, yo3)
    yrecv = (yr0, yr1, yr2, yr3)
    final = (f0, f1, f2, f3)
    outs = (gq, go, gu, gd)

    def at_piece(ref, k, zi, lead=()):
        rows = pl.ds(pl.multiple_of(zi * PIECE[k], PIECE[k]), PIECE[k])
        if k == QKV:
            return ref.at[(*lead, slice(None), rows)]
        return ref.at[(*lead, rows)]

    def y_dev(i):
        return {"s": lax.rem(s + i % 2, 2), "yh": lax.rem(yh + i // 2, 2)}

    def z_dev(d):
        return {"z": lax.rem(z + d, 4)}

    core = {"c": 1 - c}

    barrier = pltpu.get_barrier_semaphore()

    def greet(dev):
        pl.semaphore_signal(barrier, inc=1, device_id=dev, device_id_type=MESH)

    for d in (1, 2, 3):
        greet({"x": lax.rem(x + d, 4)})
        greet(z_dev(d))
        greet(y_dev(d))
    greet(core)

    @pl.when(diag)
    def _():
        pl.semaphore_wait(barrier, 10)

    @pl.when(jnp.logical_not(diag))
    def _():
        greet({"s": s, "yh": c, "c": yh})
        greet({"s": 1 - s, "yh": c, "c": yh})
        pl.semaphore_wait(barrier, 12)

    own_rows = pl.ds(pl.multiple_of((2 * x + c) * BLK, BLK), BLK)
    mirror = {"yh": c, "c": yh}
    mirror_rows = pl.ds(pl.multiple_of((2 * x + yh) * BLK, BLK), BLK)
    swaps = (
        (inp.at[s], hbuf.at[0, mirror_rows]),
        (seg.at[s], segb),
        (cot.at[s], cotb),
    )

    def swap_start(i):
        src, dst = swaps[i]

        @pl.when(diag)
        def _():
            pltpu.make_async_copy(src, dst, swap_r.at[i]).start()

        @pl.when(jnp.logical_not(diag))
        def _():
            remote(src, dst, swap_s.at[i], swap_r.at[i], mirror).start()

    def swap_wait(i):
        src, dst = swaps[i]

        @pl.when(diag)
        def _():
            pltpu.make_async_copy(src, dst, swap_r.at[i]).wait()

        @pl.when(jnp.logical_not(diag))
        def _():
            remote(src, dst, swap_s.at[i], swap_r.at[i], mirror).wait()

    def wy_copy(k, i):
        if k == 4:
            return remote(sw_in, sw.at[s], wy_s.at[k, i], wy_r.at[s, k], y_dev(i))
        src = at_piece(weights_in[k], k, z)
        return remote(src, at_piece(weights[k], k, z, (s,)), wy_s.at[k, i], wy_r.at[s, k], y_dev(i))

    def wy_arrival(l, k):
        if k == 4:
            return remote(sw_in, sw.at[l], wy_s.at[k, 0], wy_r.at[l, k], core)
        dst = at_piece(weights[k], k, z, (l,))
        return remote(dst, dst, wy_s.at[k, 0], wy_r.at[l, k], core)

    def wl_copy(k):
        if k == 4:
            return pltpu.make_async_copy(sw_in, sw.at[s], wl.at[k])
        return pltpu.make_async_copy(weights_in[k], weights[k].at[s], wl.at[k])

    def wz_copy(l, k, d):
        piece = at_piece(weights[k], k, z, (l,))
        return remote(piece, piece, wz_s.at[l, k, d], wz_r.at[l, k, d], z_dev(d))

    def wz_arrival(l, k, d):
        piece = at_piece(weights[k], k, lax.rem(z + 4 - d, 4), (l,))
        return remote(piece, piece, wz_s.at[l, k, d], wz_r.at[l, k, d], z_dev(d))

    def mine(l):
        return jnp.logical_and(diag, s == l)

    def relay(l, k):
        @pl.when(jnp.logical_not(mine(l)))
        def _():
            wy_arrival(l, k).wait_recv()
            if k != 4:
                for d in (1, 3, 2):
                    wz_copy(l, k, d).start()

    def ready(l, k):
        @pl.when(mine(l))
        def _():
            wl_copy(k).wait()

        @pl.when(jnp.logical_not(mine(l)))
        def _():
            for d in (1, 3, 2):
                wz_arrival(l, k, d).wait_recv()

    def spread(k):
        @pl.when(diag)
        def _():
            for i in (1, 3, 2):
                wy_copy(k, i).start()
            wl_copy(k).start()

    swap_start(0)
    spread(4)
    spread(QKV)
    swap_start(1)
    spread(OUT)
    spread(UP)
    spread(DOWN)
    swap_start(2)

    def arrival(i):
        return i + (i // 2) * (5 - 2 * i)

    def ag_direct(ph, view, d):
        block = view.at[own_rows]
        return remote(block, block, ag_s.at[ph, d], ag_r.at[ph, d], {"x": lax.rem(x + d, 4)})

    def ag_forward(ph, view, d):
        rows = pl.ds(pl.multiple_of((2 * lax.rem(x + 4 - d, 4) + c) * BLK, BLK), BLK)
        block = view.at[rows]
        return remote(block, block, cg_s.at[ph, d], cg_r.at[ph, d], core)

    def ag_start(ph, view):
        for d in (1, 3, 2):
            ag_direct(ph, view, d).start()
        ag_forward(ph, view, 0).start()

    def ag_block(ph, view, i):
        d = arrival(i)

        @pl.when(i > 0)
        def _():
            ag_direct(ph, view, d).wait_recv()
            ag_forward(ph, view, d).start()

        ag_forward(ph, view, d).wait_recv()
        return pl.multiple_of(lax.rem(x + 4 - d, 4) * 128, 128)

    def ag_end(ph, view):
        for d in (1, 2, 3):
            ag_direct(ph, view, d).wait_send()
        for d in range(4):
            ag_forward(ph, view, d).wait_send()

    mine64 = pl.ds(pl.multiple_of(c * BLK, BLK), BLK)
    theirs64 = pl.ds(pl.multiple_of((1 - c) * BLK, BLK), BLK)

    def ra_copy(ph, d):
        return remote(aout.at[d], ain.at[ph, d], ra_s.at[ph, d], ra_r.at[ph, d], core)

    def rb_copy(ph, d):
        return remote(
            bout.at[d], bin_.at[ph, d], rb_s.at[ph, d], rb_r.at[ph, d], {"x": lax.rem(x + 4 - d, 4)}
        )

    def rs_begin(ph, d, value):
        part[d] = value
        aout[d] = part[d, theirs64, :].astype(BF)
        ra_copy(ph, d).start()

    def rs_pass(ph, d):
        ra_copy(ph, d).wait_recv()
        total = part[d, mine64, :] + ain[ph, d].astype(F32)

        @pl.when(d == 0)
        def _():
            res[...] = total

        @pl.when(d != 0)
        def _():
            bout[d] = total.astype(BF)
            rb_copy(ph, d).start()

    def rs_loop(ph, order, step):
        def one(i, carry):
            @pl.when(i < 4)
            def _():
                d = order(i)
                rs_begin(ph, d, step(i, d))

            @pl.when(i > 0)
            def _():
                rs_pass(ph, order(i - 1))

            return carry

        lax.fori_loop(0, 5, one, 0)

    def rs_end(ph):
        total = res[...]
        for d in (1, 3, 2):
            rb_copy(ph, d).wait_recv()
            total = total + bin_[ph, d].astype(F32)
        for d in range(4):
            ra_copy(ph, d).wait_send()
        for d in (1, 2, 3):
            rb_copy(ph, d).wait_send()
        return total

    lanes = lax.broadcasted_iota(jnp.int32, (1, 128), 1) < 64
    head_mask = (
        lanes.astype(F32).astype(BF),
        (1.0 - lanes.astype(F32)).astype(BF),
    )
    first_head = lax.broadcasted_iota(jnp.int32, (128, 128), 1) < 64

    def home_copy(l, src, dst, send, recv):
        return remote(src.at[l], dst.at[s], send.at[l], recv.at[s], {"s": l, "yh": c, "c": yh})

    def home_start(l, src, dst, send, recv):
        @pl.when(mine(l))
        def _():
            dst[s] = src[l]

        @pl.when(jnp.logical_not(mine(l)))
        def _():
            home_copy(l, src, dst, send, recv).start()

    def home_wait(src, dst, send, recv):
        for l in range(2):
            @pl.when(jnp.logical_not(mine(l)))
            def _():
                home_copy(l, src, dst, send, recv).wait_send()
                remote(src.at[l], dst.at[l], send.at[l], recv.at[l], core).wait_recv()

    def reversed_arrival(i):
        return arrival(3 - i)

    swap_wait(0)
    ag_start(FA, hbuf.at[0])
    relay(0, 4)
    relay(0, QKV)
    relay(1, 4)

    @pl.when(diag)
    def _():
        wl_copy(4).wait()

    swap_wait(1)
    documents = lax.broadcasted_iota(jnp.int32, (8, SEQ), 0) == segb[...]
    documents = documents.astype(F32).astype(BF)
    bias[...] = jnp.where(dot_tn(documents, documents) > 0.5, 0.0, -1e30)

    def forward(l, carry):
        small = sw[l]
        out_b, gain_a, shift_a = small[0:1], small[1:2], small[2:3]
        down_b, gain_b, shift_b = small[3:4], small[4:5], small[5:6]
        view = hbuf.at[l]

        @pl.when(l == 1)
        def _():
            ag_start(FA, view)

        ready(l, QKV)

        def project(i, carry):
            r0 = ag_block(FA, view, i)
            rows = hbuf[l, pl.ds(r0, 128), :]
            q = dot_nn(rows, wq[l, 0]) + sw[l, 6:7, 512:640]
            k = dot_nn(rows, wq[l, 1])
            v = dot_nn(rows, wq[l, 2]) + sw[l, 6:7, 640:768]
            qkv[l, 0, pl.ds(r0, 128), :] = q.astype(BF)
            qkv[l, 1, pl.ds(r0, 128), :] = k.astype(BF)
            qkv[l, 2, pl.ds(r0, 128), :] = v.astype(BF)
            return carry

        lax.fori_loop(0, 4, project, 0)

        @pl.when(l == 0)
        def _():
            relay(0, OUT)
            relay(0, UP)

        ready(l, OUT)

        def attend(i, d):
            r0 = pl.multiple_of(lax.rem(x + 4 - d, 4) * 128, 128)
            q = qkv[l, 0, pl.ds(r0, 128), :]
            keys = qkv[l, 1]
            values = qkv[l, 2]
            heads = []
            for h in range(2):
                scores = dot_nt(q * head_mask[h], keys) * 0.125 + bias[pl.ds(r0, 128), :]
                e = jnp.exp(scores - jnp.max(scores, axis=-1, keepdims=True))
                p = (e * (1.0 / jnp.sum(e, axis=-1, keepdims=True))).astype(BF)
                probs[l, h, pl.ds(r0, 128), :] = p
                heads.append(dot_nn(p, values))
            block = jnp.where(first_head, heads[0], heads[1]).astype(BF)
            att[l, pl.ds(r0, 128), :] = block
            return dot_nn(block, wo[l])

        rs_loop(FA, reversed_arrival, attend)

        @pl.when(l == 0)
        def _():
            relay(0, DOWN)
            for k in (QKV, OUT, UP, DOWN):
                relay(1, k)

        r1 = hbuf[l, own_rows, :].astype(F32) + rs_end(FA) + out_b
        ag_end(FA, view)
        n, scale = normed(r1)
        n1[l] = n
        sc1[l] = jnp.broadcast_to(scale, (BLK, 128))
        a = n * gain_a + shift_a
        abuf[...] = a
        arbuf[l, own_rows, :] = a.astype(BF)
        ar_view = arbuf.at[l]
        ag_start(FM, ar_view)
        ready(l, UP)
        ready(l, DOWN)

        def feed(i, d):
            r0 = ag_block(FM, ar_view, i)
            u = dot_nn(arbuf[l, pl.ds(r0, 128), :], wu[l]) + sw[l, 6:7, 0:512]
            cdf = 0.5 * (1.0 + lax.erf(u * 0.7071067811865476))
            gp[l, pl.ds(r0, 128), :] = cdf + u * (jnp.exp(-0.5 * u * u) * 0.3989422804014327)
            g = (u * cdf).astype(BF)
            gr[l, pl.ds(r0, 128), :] = g
            return dot_nn(g, wd[l])

        rs_loop(FM, arrival, feed)
        r2 = abuf[...] + rs_end(FM) + down_b
        ag_end(FM, ar_view)
        n, scale = normed(r2)
        n2[l] = n
        sc2[l] = jnp.broadcast_to(scale, (BLK, 128))
        y = (n * gain_b + shift_b).astype(BF)
        yb[l] = y

        @pl.when(l == 0)
        def _():
            hbuf[1, own_rows, :] = y

        home_start(l, yb, lob, lo_s, lo_r)
        return carry

    lax.fori_loop(0, 2, forward, 0)

    def gz_copy(l, k, d):
        src = at_piece(grads[k], k, lax.rem(z + d, 4), (l,))
        return remote(src, zrecv[k].at[l, d - 1], gz_s.at[l, k, d], gz_r.at[l, k, d], z_dev(d))

    def gz_start(l, k):
        for d in (1, 3, 2):
            gz_copy(l, k, d).start()

    def gy_copy(l, k):
        slot = 2 * lax.rem(yh + 2 - c, 2) + lax.rem(s + 2 - l, 2)
        return remote(
            yout[k].at[l], yrecv[k].at[slot - 1], gy_s.at[l, k], gy_r.at[k, slot], {"s": l, "yh": c}
        )

    def gy_start(l, k):
        total = at_piece(grads[k], k, z, (l,))[...].astype(F32)
        for d in (1, 3, 2):
            gz_copy(l, k, d).wait_recv()
            total = total + zrecv[k][l, d - 1].astype(F32)
        yout[k][l] = total.astype(BF)

        @pl.when(jnp.logical_not(mine(l)))
        def _():
            gy_copy(l, k).start()

    def fz_copy(k, d):
        piece = at_piece(final[k], k, z)
        return remote(piece, piece, fz_s.at[k, d], fz_r.at[k, d], z_dev(d))

    def fc_copy(k, d):
        piece = at_piece(final[k], k, lax.rem(z + 4 - d, 4))
        return remote(piece, piece, fc_s.at[k, d], fc_r.at[k, d], core)

    def fz_start(k):
        @pl.when(diag)
        def _():
            total = yout[k][s].astype(F32)
            for i in (1, 2, 3):
                remote(
                    yrecv[k].at[i - 1], yrecv[k].at[i - 1], gy_s.at[0, k], gy_r.at[k, i], core
                ).wait_recv()
                total = total + yrecv[k][i - 1].astype(F32)
            at_piece(final[k], k, z)[...] = total.astype(BF)
            for d in (1, 3, 2):
                fz_copy(k, d).start()
            fc_copy(k, 0).start()

    def fc_start(k):
        @pl.when(diag)
        def _():
            for d in (1, 3, 2):
                piece = at_piece(final[k], k, lax.rem(z + 4 - d, 4))
                remote(piece, piece, fz_s.at[k, d], fz_r.at[k, d], z_dev(d)).wait_recv()
                fc_copy(k, d).start()

    def out_start(k):
        @pl.when(jnp.logical_not(diag))
        def _():
            for d in range(4):
                fc_copy(k, d).wait_recv()

        pltpu.make_async_copy(final[k], outs[k], st.at[k]).start()

    swap_wait(2)

    def backward(step_index, carry):
        l = 1 - step_index
        small = sw[l]
        gain_a, gain_b = small[1:2], small[4:5]

        @pl.when(l == 1)
        def _():
            res[...] = cotb[...].astype(F32)

        @pl.when(l == 0)
        def _():
            res[...] = dhb[1].astype(F32)

        dy = res[...]
        n = n2[l]
        dr2 = norm_back(dy, gain_b, n, sc2[l, :, 0:1])
        dmbuf[own_rows, :] = dr2.astype(BF)
        ag_start(BM, dmbuf)
        gsb[l] = jnp.zeros((8, D), F32)
        gsb[l, 4:5, :] = col_sum(dy * n)
        gsb[l, 5:6, :] = col_sum(dy)
        gsb[l, 3:4, :] = col_sum(dr2)
        abuf[...] = dr2

        def feed_back(i, d):
            r0 = ag_block(BM, dmbuf, i)
            dg = dot_nt(dmbuf[pl.ds(r0, 128), :], wd[l])
            du = dg * gp[l, pl.ds(r0, 128), :]
            gsb[l, 6:7, 0:512] += col_sum(du)
            low = du.astype(BF)
            dur[pl.ds(r0, 128), :] = low
            return dot_nt(low, wu[l])

        rs_loop(BM, arrival, feed_back)

        def grad_down(i, carry):
            cols = pl.ds(pl.multiple_of(i * 128, 128), 128)
            g3[l, cols, :] = dot_tn(gr[l, :, cols], dmbuf[...]).astype(BF)
            return carry

        lax.fori_loop(0, 4, grad_down, 0)
        gz_start(l, DOWN)

        def grad_up(i, carry):
            cols = pl.ds(pl.multiple_of(i * 128, 128), 128)
            g2[l, cols, :] = dot_tn(arbuf[l, :, cols], dur[...]).astype(BF)
            return carry

        lax.fori_loop(0, 8, grad_up, 0)
        gz_start(l, UP)
        da = abuf[...] + rs_end(BM)
        ag_end(BM, dmbuf)
        n = n1[l]
        dr1 = norm_back(da, gain_a, n, sc1[l, :, 0:1])
        dprbuf[own_rows, :] = dr1.astype(BF)
        ag_start(BA, dprbuf)
        gsb[l, 1:2, :] = col_sum(da * n)
        gsb[l, 2:3, :] = col_sum(da)
        gsb[l, 0:1, :] = col_sum(dr1)
        abuf[...] = dr1
        dacc[...] = jnp.zeros_like(dacc)

        @pl.when(l == 0)
        def _():
            for k in (DOWN, UP):
                gy_start(1, k)

        def attend_back(i, carry):
            r0 = ag_block(BA, dprbuf, i)
            rows = pl.ds(r0, 128)
            grad = dot_nt(dprbuf[rows, :], wo[l]).astype(BF)
            q = qkv[l, 0, rows, :]
            keys = qkv[l, 1]
            values = qkv[l, 2]
            heads = []
            dk = dacc[0]
            dv = dacc[1]
            for h in range(2):
                own = grad * head_mask[h]
                low_p = probs[l, h, rows, :]
                p = low_p.astype(F32)
                dp = dot_nt(own, values)
                ds = (p * (dp - jnp.sum(p * dp, axis=-1, keepdims=True))).astype(BF)
                heads.append(dot_nn(ds, keys))
                dk = dk + dot_tn(ds, q * head_mask[h])
                dv = dv + dot_tn(low_p, own)
            dacc[0] = dk
            dacc[1] = dv
            dq = (jnp.where(first_head, heads[0], heads[1]) * 0.125).astype(BF)
            dx[0, rows, :] = dq
            gsb[l, 6:7, 512:640] += col_sum(dq.astype(F32))
            return carry

        lax.fori_loop(0, 4, attend_back, 0)
        dx[1] = (dacc[0] * 0.125).astype(BF)
        dv = dacc[1].astype(BF)
        dx[2] = dv
        gsb[l, 6:7, 640:768] = col_sum(dv.astype(F32))

        def input_back(i, d):
            rows = pl.ds(pl.multiple_of(lax.rem(x + 4 - d, 4) * 128, 128), 128)
            return (
                dot_nt(dx[0, rows, :], wq[l, 0])
                + dot_nt(dx[1, rows, :], wq[l, 1])
                + dot_nt(dx[2, rows, :], wq[l, 2])
            )

        rs_loop(BA, reversed_arrival, input_back)

        def grad_qkv(i, carry):
            cols = pl.ds(pl.multiple_of(i * 128, 128), 128)
            rows = hbuf[l, :, cols]
            for j in range(3):
                g0[l, j, cols, :] = dot_tn(rows, dx[j]).astype(BF)
            return carry

        lax.fori_loop(0, 8, grad_qkv, 0)
        gz_start(l, QKV)
        g1[l] = dot_tn(att[l], dprbuf[...]).astype(BF)
        gz_start(l, OUT)
        dh = (abuf[...] + rs_end(BA)).astype(BF)
        ag_end(BA, dprbuf)
        dhb[l] = dh
        home_start(l, dhb, igb, ig_s, ig_r)
        return carry

    lax.fori_loop(0, 2, backward, 0)

    small_out = pltpu.make_async_copy(gsb, gs, st.at[4])
    small_out.start()
    for k in (QKV, OUT):
        gy_start(1, k)
    for k in (DOWN, UP):
        gy_start(0, k)
    for k in (DOWN, UP):
        fz_start(k)
    for k in (QKV, OUT):
        gy_start(0, k)
    for k in (DOWN, UP):
        fc_start(k)
    for k in (QKV, OUT):
        fz_start(k)
    home_wait(yb, lob, lo_s, lo_r)
    lo_out = pltpu.make_async_copy(lob, lo, st.at[5])
    lo_out.start()
    home_wait(dhb, igb, ig_s, ig_r)
    ig_out = pltpu.make_async_copy(igb, ig, st.at[6])
    ig_out.start()
    for k in (DOWN, UP):
        out_start(k)
    for k in (QKV, OUT):
        fc_start(k)
    for k in (QKV, OUT):
        out_start(k)

    @pl.when(diag)
    def _():
        for k in range(5):
            for i in (1, 2, 3):
                wy_copy(k, i).wait_send()

    for l in range(2):
        for k in range(4):
            @pl.when(jnp.logical_not(mine(l)))
            def _():
                for d in (1, 2, 3):
                    wz_copy(l, k, d).wait_send()
                gy_copy(l, k).wait_send()

            for d in (1, 2, 3):
                gz_copy(l, k, d).wait_send()

    @pl.when(diag)
    def _():
        for k in range(4):
            for d in (1, 2, 3):
                fz_copy(k, d).wait_send()
            for d in range(4):
                fc_copy(k, d).wait_send()

    small_out.wait()
    lo_out.wait()
    ig_out.wait()
    for k in range(4):
        pltpu.make_async_copy(final[k], outs[k], st.at[k]).wait()


WSHAPES = ((3, D, 128), (128, D), (D, FFS), (FFS, D))
PSHAPES = ((3, 256, 128), (32, D), (256, FFS), (128, D))


def run(inp, cot, seg, wq, wo, wu, wd, sw):
    vm = pltpu.VMEM
    scratch = [vm((2, *shape), BF) for shape in WSHAPES]
    scratch += [vm((2, 8, D), F32)]
    scratch += [vm((2, SEQ, D), BF)] * 2 + [vm((SEQ, D), BF)] * 2
    scratch += [vm((4, 4, BLK, D), BF)] * 2 + [vm((4, BLK, D), BF)] * 2 + [vm((4, 128, D), F32)]
    scratch += [
        vm((2, 3, SEQ, 128), BF),
        vm((2, SEQ, 128), BF),
        vm((2, 2, SEQ, SEQ), BF),
        vm((2, SEQ, FFS), F32),
        vm((2, SEQ, FFS), BF),
        vm((2, BLK, D), F32),
        vm((2, BLK, D), F32),
        vm((2, BLK, 128), F32),
        vm((2, BLK, 128), F32),
        vm((BLK, D), F32),
        vm((BLK, D), F32),
    ]
    scratch += [
        vm((8, SEQ), jnp.int32),
        vm((SEQ, SEQ), F32),
        vm((BLK, D), BF),
        vm((SEQ, FFS), BF),
        vm((2, SEQ, 128), F32),
        vm((3, SEQ, 128), BF),
    ]
    scratch += [vm((2, BLK, D), BF)] * 4 + [vm((2, 8, D), F32)]
    scratch += [vm((2, *shape), BF) for shape in WSHAPES]
    scratch += [vm((2, 3, *shape), BF) for shape in PSHAPES]
    scratch += [vm((2, *shape), BF) for shape in PSHAPES]
    scratch += [vm((3, *shape), BF) for shape in PSHAPES]
    scratch += [vm(shape, BF) for shape in WSHAPES]
    dma = pltpu.SemaphoreType.DMA
    scratch += [dma((3,)), dma((3,)), dma((5, 4)), dma((2, 5)), dma((2, 4, 4)), dma((2, 4, 4)), dma((5,))]
    scratch += [dma((4, 4))] * 8
    scratch += [dma((2,))] * 4
    scratch += [dma((2, 4, 4)), dma((2, 4, 4)), dma((2, 4)), dma((4, 4))]
    scratch += [dma((4, 4))] * 4 + [dma((7,))]
    any_space = pl.BlockSpec(memory_space=pl.ANY)
    return pl.pallas_call(
        kernel,
        out_shape=[
            jax.ShapeDtypeStruct((2, BLK, D), BF),
            jax.ShapeDtypeStruct((2, BLK, D), BF),
            *(jax.ShapeDtypeStruct(shape, BF) for shape in WSHAPES),
            jax.ShapeDtypeStruct((2, 8, D), F32),
        ],
        in_specs=[any_space] * 8,
        out_specs=[any_space] * 7,
        scratch_shapes=scratch,
        compiler_params=pltpu.CompilerParams(
            collective_id=0, has_side_effects=True, vmem_limit_bytes=60 * 1024 * 1024
        ),
    )(inp, cot, seg, wq, wo, wu, wd, sw)


def local(
    inputs, segments, qkv_weight, qv_bias, out_weight, out_bias, gain_one, shift_one,
    up_weight, up_bias, down_weight, down_bias, gain_two, shift_two, cotangent,
):
    x = lax.axis_index("x")
    yh = lax.axis_index("yh")
    s = lax.axis_index("s")
    c = lax.axis_index("c")
    mixed = jnp.concatenate(
        [up_bias.astype(F32), qv_bias.reshape(1, 256).astype(F32), jnp.zeros((1, 256), F32)], axis=1
    )
    small = jnp.concatenate(
        [v.astype(F32) for v in (out_bias, gain_one, shift_one, down_bias, gain_two, shift_two)]
        + [mixed, jnp.zeros((1, D), F32)],
        axis=0,
    )
    seg = jnp.broadcast_to(segments, (2, 8, SEQ))
    lo, ig, gq, go, gu, gd, gs = run(
        inputs[:, 0], cotangent[:, 0], seg,
        qkv_weight[0], out_weight[0], up_weight[0], down_weight[0], small,
    )
    slot = (lax.broadcasted_iota(jnp.int32, (8, 1, 1), 0) == 2 * x + c).astype(F32)
    mixed_sums = slot * gs[None, :, 6, :768]
    wide, mixed_sums = lax.psum((gs[:, :6], mixed_sums), ("s", "x", "yh", "z", "c"))
    wide = lax.dynamic_index_in_dim(wide, s, 0, keepdims=False)
    mixed_sums = lax.dynamic_index_in_dim(mixed_sums, 2 * x + yh, 0, keepdims=False)
    mixed_sums = lax.dynamic_index_in_dim(mixed_sums, s, 0, keepdims=True)
    return (
        lo[None, :, None],
        ig[None, :, None],
        gq[None].astype(F32),
        mixed_sums[:, 512:768].reshape(1, 2, 128),
        go[None].astype(F32),
        wide[0:1],
        wide[1:2],
        wide[2:3],
        gu[None].astype(F32),
        mixed_sums[:, 0:512],
        gd[None].astype(F32),
        wide[3:4],
        wide[4:5],
        wide[5:6],
    )


def solution(mesh):
    fine = Mesh(mesh.devices.reshape(2, 4, 2, 4, 2), ("s", "x", "yh", "z", "c"))
    t = ("x", "yh")
    dp = ("z", "c")
    return jax.shard_map(
        local,
        mesh=fine,
        in_specs=(
            P(None, dp, t, None),
            P(None, dp, None),
            P("s", None, None, t),
            P("s", None, t),
            P("s", t, None),
            P("s", None),
            P("s", None),
            P("s", None),
            P("s", None, t),
            P("s", t),
            P("s", t, None),
            P("s", None),
            P("s", None),
            P("s", None),
            P(None, dp, t, None),
        ),
        out_specs=(
            P("s", None, dp, t, None),
            P("s", None, dp, t, None),
            P("s", None, None, t),
            P("s", None, t),
            P("s", t, None),
            P("s", None),
            P("s", None),
            P("s", None),
            P("s", None, t),
            P("s", t),
            P("s", t, None),
            P("s", None),
            P("s", None),
            P("s", None),
        ),
        check_vma=False,
    )
```

time: 1920 us -> 404 us (0.21)
  waiting for transfers between devices: 1310 us -> 131 us
  blocking collectives: 340 us -> 0 us
  Pallas kernels: 0 us -> 242 us
  matrix products: 113 us -> 0 us
  other arithmetic: 81.1 us -> 8.55 us
  local copies, waits for them, and re-layouts: 37.7 us -> 8.52 us
    reduce_scatter x12 -> x0, waiting for transfers between devices: 749 us -> none  [the longest x3 210 us: layer_forward(): lax.psum_scatter(partial_value.astype(jnp.bfloat16), 'tensor', scatter_di...]
    all_gather x12 -> x0, waiting for transfers between devices: 548 us -> none  [the longest x3 145 us: layer_forward(): gathered = lax.all_gather(layer_in, 'tensor', axis=1, tiled=True)]
    psum x2 -> x0, blocking collectives: 340 us -> none  [the longest x1 320 us: local(): lax.psum((small_attn[0], small_attn[1], small_attn[2], small_mlp[0], smal...]
    pallas_call x0 -> x1, Pallas kernels: none -> 242 us  [run(): pl.pallas_call(kernel, out_shape=[jax.ShapeDtypeStruct((2, BLK, D), BF),...]
    psum x1, waiting for transfers between devices: 0.01 us -> 131 us  [local(): lax.psum((gs[:, :6], mixed_sums), ('s', 'x', 'yh', 'z', 'c'))]
    dot_general x54 -> x0, matrix products: 107 us -> none  [the longest x9 26.8 us: contract_cols(): lax.dot_general(left, right, (((1,), (1,)), ((), ())), preferred_element_...]
    reduce_sum x31 -> x0, other arithmetic: 30.4 us -> none  [the longest x13 14.2 us: layer_norm(): center = values - jnp.mean(values, axis=-1, keepdims=True)]
    unnamed x365 -> x14, local copies, waits for them, and re-layouts: 21.3 us -> 2.12 us
  transfers between devices with their start and end apart: 29 -> 1, of which waited for: 27 -> 1; matrix products, arithmetic and copies ran while one was open for 3% -> 2% of each run, Pallas kernels for 0% -> 0%
where the time goes in v1:
time: 404 us
  Pallas kernels  242 us (60%)
  waiting for transfers between devices  131 us (32%)
  between operations  14.1 us (3%)
  other arithmetic  8.55 us (2%)
  local copies, waits for them, and re-layouts  8.52 us (2%)
    pallas_call x1, Pallas kernels, run(): pl.pallas_call(kernel, out_shape=[jax.ShapeDtypeStruct((2, BLK, D), BF),...  242 us
    psum x1, waiting for transfers between devices, local(): lax.psum((gs[:, :6], mixed_sums), ('s', 'x', 'yh', 'z', 'c'))  131 us
  transfers between devices with their start and end apart: 1, of which 1 were waited for; matrix products, arithmetic and copies ran while one was open for 2% of the time, Pallas kernels for 0%

profile of v1, /device:TPU:1, one launch (start us, length us, event | category | flops | bytes accessed | tf_op | source)
XLA Modules:
  0.0 403.7 jit_solution(13754787505954252522)
XLA Ops:
  7.2 0.0 all-reduce.3.cloned.1.call-start
  7.2 0.7 convert_element_type.73
  7.9 0.7 convert_element_type.85
  8.6 0.7 copy.36
  9.3 1.4 concatenate.7.sw_in
  10.7 0.6 broadcast_in_dim.24.seg
  11.4 241.9 %shard_map.254 = (bf16[2,64,1024]{2,1,0:T(8,128)(2,1)}, bf16[2,64,1024]{2,1,0:T(8,128)(2,1)}, bf16[3,1024,128]{2,1,0:T(8,128)(2,1)}, bf16[128,1024]{1,0:T(8,128)...) custom-call(bf16[2,64,1024]{2,1,0:T(8,128)(2,1)} %bitcast.51, ...), custom_call_target="tpu_custom_call" | custom-call | tf_op jit(solution)/shard_map/pallas_call | solution.py:744
  253.3 0.0 copy-start
  253.3 0.9 slice.48
  254.2 0.7 broadcast_multiply_fusion
  254.9 0.0 all-reduce.3.cloned.1.call-update
  254.9 2.8 bitcast_convert_fusion
  257.7 0.0 copy-start.1
  257.7 0.0 copy-done
  257.7 0.0 copy-start.2
  257.7 1.6 bitcast_convert_fusion.1
  259.4 0.0 copy-start.4
  259.4 0.0 copy-start.3
  259.4 0.0 copy-done.1
  259.4 1.2 bitcast_convert_fusion.2
  260.6 0.0 copy-done.2
  260.6 0.8 bitcast_convert_fusion.3
  261.4 130.5 %all-reduce.3.cloned.1.call-done = (f32[8,2,768]{2,1,0:T(2,128)}, f32[2,6,1024]{2,1,0:T(8,128)}) async-done(((f32[8,2,768]{2,1,0:T(2,128)}, f32[2,6,1024]{2,1,0:T(8,128)}), (f32[8,2,768]{2,1,0:T(2,128)}, f32[2,6,1024]{2,1,0:T(8,128)})) %all-reduce.3.cloned.1.call-update) | async-done | bytes 98320 | tf_op jit(solution)/shard_map/psum | solution.py:784
  392.0 0.7 dynamic-slice_bitcast_fusion.6
  392.7 0.6 slice.65
  393.3 0.6 slice.64
  393.8 1.6 dynamic-slice_bitcast_fusion
  395.4 0.0 copy-done.4
  395.4 0.7 copy.41
  396.1 0.0 copy-done.3
  396.1 0.7 copy.42
  (6 shorter events, 0.0 us)
Async XLA Ops:
  7.2 384.8 %all-reduce.3.cloned.1.call-start = ((), (), s32[]{:S(2)}) async-start(), calls=%async_computation | async-start | bytes 229376 | tf_op jit(solution)/shard_map/psum | solution.py:784
  253.3 4.5 %copy-start = (bf16[1024,512]{1,0:T(8,128)(2,1)S(1)}, bf16[1024,512]{1,0:T(8,128)(2,1)}, u32[]{:S(2)}) copy-start(bf16[1024,512]{1,0:T(8,128)(2,1)} %get-tuple-element.26) | copy-start | bytes 3145732
  257.7 1.6 copy-start.1
  257.7 2.9 copy-start.2
  259.4 136.1 %copy-start.4 = (bf16[2,64,1024]{2,1,0:T(8,128)(2,1)S(1)}, bf16[2,64,1024]{2,1,0:T(8,128)(2,1)}, u32[]{:S(2)}) copy-start(bf16[2,64,1024]{2,1,0:T(8,128)(2,1)} %get-tuple-element.21) | copy-start | bytes 786436
  259.4 136.8 %copy-start.3 = (bf16[2,64,1024]{2,1,0:T(8,128)(2,1)S(1)}, bf16[2,64,1024]{2,1,0:T(8,128)(2,1)}, u32[]{:S(2)}) copy-start(bf16[2,64,1024]{2,1,0:T(8,128)(2,1)} %get-tuple-element.22) | copy-start | bytes 786436
Sparse Core Ops, SparseCore 0:
  255.1 136.8 all-reduce.2

commit v2 on v1

--- a/solution.py
+++ b/solution.py
@@ -55,14 +55,16 @@
 
 
 def kernel(
-    inp, cot, seg, wq_in, wo_in, wu_in, wd_in, sw_in,
+    inp, cot, seg_in, wq_in, wo_in, wu_in, wd_in,
+    ob_in, ga_in, sa_in, db_in, gb_in, sb_in, ub_in, qb_in,
     lo, ig, gq, go, gu, gd, gs,
+    sw_in, seg,
     wq, wo, wu, wd, sw,
     hbuf, arbuf, dmbuf, dprbuf,
     ain, bin_, aout, bout, part,
     qkv, att, probs, gp, gr, n1, n2, sc1, sc2, abuf, res,
     segb, bias, cotb, dur, dacc, dx,
-    yb, lob, dhb, igb, gsb,
+    yb, lob, dhb, igb, gsb, sx, sc, sz, sy, gsout,
     g0, g1, g2, g3,
     zr0, zr1, zr2, zr3,
     yo0, yo1, yo2, yo3,
@@ -71,7 +73,7 @@
     swap_s, swap_r, wy_s, wy_r, wz_s, wz_r, wl,
     ag_s, ag_r, cg_s, cg_r, ra_s, ra_r, rb_s, rb_r,
     lo_s, lo_r, ig_s, ig_r,
-    gz_s, gz_r, gy_s, gy_r, fz_s, fz_r, fc_s, fc_r, st,
+    gz_s, gz_r, gy_s, gy_r, fz_s, fz_r, fc_s, fc_r, st, sx_s, sx_r, sc_s, sc_r, sz_s, sz_r, sy_s, sy_r,
 ):
     s = lax.axis_index("s")
     x = lax.axis_index("x")
@@ -102,6 +104,14 @@
 
     core = {"c": 1 - c}
 
+    for i, ref in enumerate((ob_in, ga_in, sa_in, db_in, gb_in, sb_in)):
+        sw_in[i : i + 1, :] = ref[...].astype(F32)
+    sw_in[6:7, 0:512] = ub_in[...].astype(F32)
+    sw_in[6:7, 512:640] = qb_in[0, 0:1, :].astype(F32)
+    sw_in[6:7, 640:768] = qb_in[0, 1:2, :].astype(F32)
+    for m in range(2):
+        seg[m] = jnp.broadcast_to(seg_in[m], (8, SEQ))
+
     barrier = pltpu.get_barrier_semaphore()
 
     def greet(dev):
@@ -507,6 +517,56 @@
                 fc_copy(k, d).wait_recv()
 
         pltpu.make_async_copy(final[k], outs[k], st.at[k]).start()
+
+    def sx_copy(l, d):
+        return remote(gsb.at[l], sx.at[l, x], sx_s.at[l, d], sx_r.at[l, d], {"x": lax.rem(x + d, 4)})
+
+    def sc_copy(l):
+        return remote(sc.at[l, c], sc.at[l, c], sc_s.at[l], sc_r.at[l], core)
+
+    def sz_copy(l, d):
+        return remote(sz.at[l, z], sz.at[l, z], sz_s.at[l, d], sz_r.at[l, d], z_dev(d))
+
+    def sy_copy(l, i):
+        block = sy.at[l, 2 * yh + s]
+        return remote(block, block, sy_s.at[l, i], sy_r.at[l, i], y_dev(i))
+
+    def small_x(l):
+        sx[l, x] = gsb[l]
+        for d in (1, 3, 2):
+            sx_copy(l, d).start()
+
+    def small_core(l):
+        for d in (1, 3, 2):
+            sx_copy(l, d).wait_recv()
+        sc[l, c] = ((sx[l, 0] + sx[l, 1]) + sx[l, 2]) + sx[l, 3]
+        sc[l, c, 6:7, :] = gsb[l, 6:7, :]
+        sc_copy(l).start()
+
+    def small_z(l):
+        sc_copy(l).wait_recv()
+        sz[l, z] = sc[l, 0] + sc[l, 1]
+        sz[l, z, 6:7, :] = sc[l, 0, 6:7, :]
+        sz[l, z, 7:8, :] = sc[l, 1, 6:7, :]
+        for d in (1, 3, 2):
+            sz_copy(l, d).start()
+
+    def small_y(l):
+        for d in (1, 3, 2):
+            sz_copy(l, d).wait_recv()
+        sy[l, 2 * yh + s] = ((sz[l, 0] + sz[l, 1]) + sz[l, 2]) + sz[l, 3]
+        for i in (1, 3, 2):
+            sy_copy(l, i).start()
+
+    def small_end():
+        for l in range(2):
+            for i in (1, 3, 2):
+                sy_copy(l, i).wait_recv()
+        gsout[...] = ((sy[s, 0] + sy[s, 1]) + sy[s, 2]) + sy[s, 3]
+
+        @pl.when(yh == 1)
+        def _():
+            gsout[6:7, :] = gsout[7:8, :]
 
     swap_wait(2)
 
@@ -608,6 +668,7 @@
         dv = dacc[1].astype(BF)
         dx[2] = dv
         gsb[l, 6:7, 640:768] = col_sum(dv.astype(F32))
+        small_x(l)
 
         def input_back(i, d):
             rows = pl.ds(pl.multiple_of(lax.rem(x + 4 - d, 4) * 128, 128), 128)
@@ -618,6 +679,7 @@
             )
 
         rs_loop(BA, reversed_arrival, input_back)
+        small_core(l)
 
         def grad_qkv(i, carry):
             cols = pl.ds(pl.multiple_of(i * 128, 128), 128)
@@ -630,16 +692,16 @@
         gz_start(l, QKV)
         g1[l] = dot_tn(att[l], dprbuf[...]).astype(BF)
         gz_start(l, OUT)
+        small_z(l)
         dh = (abuf[...] + rs_end(BA)).astype(BF)
         ag_end(BA, dprbuf)
         dhb[l] = dh
         home_start(l, dhb, igb, ig_s, ig_r)
+        small_y(l)
         return carry
 
     lax.fori_loop(0, 2, backward, 0)
 
-    small_out = pltpu.make_async_copy(gsb, gs, st.at[4])
-    small_out.start()
     for k in (QKV, OUT):
         gy_start(1, k)
     for k in (DOWN, UP):
@@ -658,6 +720,9 @@
     home_wait(dhb, igb, ig_s, ig_r)
     ig_out = pltpu.make_async_copy(igb, ig, st.at[6])
     ig_out.start()
+    small_end()
+    small_out = pltpu.make_async_copy(gsout, gs, st.at[4])
+    small_out.start()
     for k in (DOWN, UP):
         out_start(k)
     for k in (QKV, OUT):
@@ -682,6 +747,12 @@
             for d in (1, 2, 3):
                 gz_copy(l, k, d).wait_send()
 
+        for d in (1, 2, 3):
+            sx_copy(l, d).wait_send()
+            sz_copy(l, d).wait_send()
+            sy_copy(l, d).wait_send()
+        sc_copy(l).wait_send()
+
     @pl.when(diag)
     def _():
         for k in range(4):
@@ -701,9 +772,10 @@
 PSHAPES = ((3, 256, 128), (32, D), (256, FFS), (128, D))
 
 
-def run(inp, cot, seg, wq, wo, wu, wd, sw):
+def run(*operands):
     vm = pltpu.VMEM
-    scratch = [vm((2, *shape), BF) for shape in WSHAPES]
+    scratch = [vm((8, D), F32), vm((2, 8, SEQ), jnp.int32)]
+    scratch += [vm((2, *shape), BF) for shape in WSHAPES]
     scratch += [vm((2, 8, D), F32)]
     scratch += [vm((2, SEQ, D), BF)] * 2 + [vm((SEQ, D), BF)] * 2
     scratch += [vm((4, 4, BLK, D), BF)] * 2 + [vm((4, BLK, D), BF)] * 2 + [vm((4, 128, D), F32)]
@@ -729,6 +801,7 @@
         vm((3, SEQ, 128), BF),
     ]
     scratch += [vm((2, BLK, D), BF)] * 4 + [vm((2, 8, D), F32)]
+    scratch += [vm((2, n, 8, D), F32) for n in (4, 2, 4, 4)] + [vm((8, D), F32)]
     scratch += [vm((2, *shape), BF) for shape in WSHAPES]
     scratch += [vm((2, 3, *shape), BF) for shape in PSHAPES]
     scratch += [vm((2, *shape), BF) for shape in PSHAPES]
@@ -740,66 +813,50 @@
     scratch += [dma((2,))] * 4
     scratch += [dma((2, 4, 4)), dma((2, 4, 4)), dma((2, 4)), dma((4, 4))]
     scratch += [dma((4, 4))] * 4 + [dma((7,))]
+    scratch += [dma((2, 4))] * 2 + [dma((2,))] * 2 + [dma((2, 4))] * 4
     any_space = pl.BlockSpec(memory_space=pl.ANY)
+    in_vmem = pl.BlockSpec(memory_space=pltpu.VMEM)
     return pl.pallas_call(
         kernel,
         out_shape=[
             jax.ShapeDtypeStruct((2, BLK, D), BF),
             jax.ShapeDtypeStruct((2, BLK, D), BF),
             *(jax.ShapeDtypeStruct(shape, BF) for shape in WSHAPES),
-            jax.ShapeDtypeStruct((2, 8, D), F32),
+            jax.ShapeDtypeStruct((8, D), F32),
         ],
-        in_specs=[any_space] * 8,
+        in_specs=[any_space] * 2 + [in_vmem] + [any_space] * 4 + [in_vmem] * 8,
         out_specs=[any_space] * 7,
         scratch_shapes=scratch,
         compiler_params=pltpu.CompilerParams(
             collective_id=0, has_side_effects=True, vmem_limit_bytes=60 * 1024 * 1024
         ),
-    )(inp, cot, seg, wq, wo, wu, wd, sw)
+    )(*operands)
 
 
 def local(
     inputs, segments, qkv_weight, qv_bias, out_weight, out_bias, gain_one, shift_one,
     up_weight, up_bias, down_weight, down_bias, gain_two, shift_two, cotangent,
 ):
-    x = lax.axis_index("x")
-    yh = lax.axis_index("yh")
-    s = lax.axis_index("s")
-    c = lax.axis_index("c")
-    mixed = jnp.concatenate(
-        [up_bias.astype(F32), qv_bias.reshape(1, 256).astype(F32), jnp.zeros((1, 256), F32)], axis=1
+    lo, ig, gq, go, gu, gd, gs = run(
+        inputs[:, 0], cotangent[:, 0], segments,
+        qkv_weight[0], out_weight[0], up_weight[0], down_weight[0],
+        out_bias, gain_one, shift_one, down_bias, gain_two, shift_two, up_bias, qv_bias,
     )
-    small = jnp.concatenate(
-        [v.astype(F32) for v in (out_bias, gain_one, shift_one, down_bias, gain_two, shift_two)]
-        + [mixed, jnp.zeros((1, D), F32)],
-        axis=0,
-    )
-    seg = jnp.broadcast_to(segments, (2, 8, SEQ))
-    lo, ig, gq, go, gu, gd, gs = run(
-        inputs[:, 0], cotangent[:, 0], seg,
-        qkv_weight[0], out_weight[0], up_weight[0], down_weight[0], small,
-    )
-    slot = (lax.broadcasted_iota(jnp.int32, (8, 1, 1), 0) == 2 * x + c).astype(F32)
-    mixed_sums = slot * gs[None, :, 6, :768]
-    wide, mixed_sums = lax.psum((gs[:, :6], mixed_sums), ("s", "x", "yh", "z", "c"))
-    wide = lax.dynamic_index_in_dim(wide, s, 0, keepdims=False)
-    mixed_sums = lax.dynamic_index_in_dim(mixed_sums, 2 * x + yh, 0, keepdims=False)
-    mixed_sums = lax.dynamic_index_in_dim(mixed_sums, s, 0, keepdims=True)
     return (
         lo[None, :, None],
         ig[None, :, None],
         gq[None].astype(F32),
-        mixed_sums[:, 512:768].reshape(1, 2, 128),
+        gs[6, 512:768].reshape(1, 2, 128),
         go[None].astype(F32),
-        wide[0:1],
-        wide[1:2],
-        wide[2:3],
+        gs[0:1],
+        gs[1:2],
+        gs[2:3],
         gu[None].astype(F32),
-        mixed_sums[:, 0:512],
+        gs[6:7, 0:512],
         gd[None].astype(F32),
-        wide[3:4],
-        wide[4:5],
-        wide[5:6],
+        gs[3:4],
+        gs[4:5],
+        gs[5:6],
     )
 
 

time: 404 us -> 283 us (0.70)
  waiting for transfers between devices: 131 us -> 0 us
  Pallas kernels: 242 us -> 270 us
  between operations: 14.1 us -> 0.68 us
    psum x1 -> x0, waiting for transfers between devices: 131 us -> none  [local(): lax.psum((gs[:, :6], mixed_sums), ('s', 'x', 'yh', 'z', 'c'))]
    pallas_call x1, Pallas kernels: 242 us -> 270 us  [run(): pl.pallas_call(kernel, out_shape=[jax.ShapeDtypeStruct((2, BLK, D), BF),...]
  transfers between devices with their start and end apart: 1 -> 0, of which waited for: 1 -> 0; matrix products, arithmetic and copies ran while one was open for 2% -> 0% of each run, Pallas kernels for 0% -> 0%
where the time goes in v2:
time: 283 us
  Pallas kernels  270 us (95%)
  other arithmetic  6.49 us (2%)
  local copies, waits for them, and re-layouts  5.69 us (2%)
    pallas_call x1, Pallas kernels, run(): pl.pallas_call(kernel, out_shape=[jax.ShapeDtypeStruct((2, BLK, D), BF),...  270 us

profile of v2, /device:TPU:1, one launch (start us, length us, event | category | flops | bytes accessed | tf_op | source)
XLA Modules:
  0.0 282.6 jit_solution(3066071750024317767)
XLA Ops:
  0.7 269.8 %shard_map.254 = (bf16[2,64,1024]{2,1,0:T(8,128)(2,1)}, bf16[2,64,1024]{2,1,0:T(8,128)(2,1)}, bf16[3,1024,128]{2,1,0:T(8,128)(2,1)}, bf16[128,1024]{1,0:T(8,128)...) custom-call(bf16[2,64,1024]{2,1,0:T(8,128)(2,1)} %bitcast.28, ...), custom_call_target="tpu_custom_call" | custom-call | tf_op jit(solution)/shard_map/pallas_call | solution.py:819
  270.4 0.0 copy-start
  270.4 1.7 fusion
  272.1 1.3 slice.28
  273.4 1.3 slice.24
  274.7 2.8 bitcast_convert_fusion
  277.5 0.0 copy-start.1
  277.5 0.0 copy-done
  277.5 0.0 copy-start.2
  277.5 1.6 bitcast_convert_fusion.1
  279.1 0.0 copy-start.4
  279.1 0.0 copy-start.3
  279.1 0.0 copy-done.1
  279.1 1.2 bitcast_convert_fusion.2
  280.4 0.0 copy-done.2
  280.4 0.8 bitcast_convert_fusion.3
  281.2 0.0 copy-done.4
  281.2 0.7 copy.33
  281.9 0.0 copy-done.3
  281.9 0.7 copy.34
Async XLA Ops:
  270.4 7.1 %copy-start = (bf16[1024,512]{1,0:T(8,128)(2,1)S(1)}, bf16[1024,512]{1,0:T(8,128)(2,1)}, u32[]{:S(2)}) copy-start(bf16[1024,512]{1,0:T(8,128)(2,1)} %get-tuple-element.26) | copy-start | bytes 3145732
  277.5 1.6 copy-start.1
  277.5 2.9 %copy-start.2 = (bf16[128,1024]{1,0:T(8,128)(2,1)S(1)}, bf16[128,1024]{1,0:T(8,128)(2,1)}, u32[]{:S(2)}) copy-start(bf16[128,1024]{1,0:T(8,128)(2,1)} %get-tuple-element.25) | copy-start | bytes 786436
  279.1 2.1 copy-start.4
  279.1 2.8 copy-start.3

commit v3 on v2

--- a/solution.py
+++ b/solution.py
@@ -14,6 +14,7 @@
 FFS = 512
 SEQ = 512
 BLK = 64
+HALF = 32
 QKV, OUT, UP, DOWN = 0, 1, 2, 3
 PIECE = (256, 32, 256, 128)
 FA, FM, BM, BA = 0, 1, 2, 3
@@ -62,7 +63,7 @@
     wq, wo, wu, wd, sw,
     hbuf, arbuf, dmbuf, dprbuf,
     ain, bin_, aout, bout, part,
-    qkv, att, probs, gp, gr, n1, n2, sc1, sc2, abuf, res,
+    qkv, att, probs, gp, gr, n1, n2, sc1, sc2, abuf, res, dyb,
     segb, bias, cotb, dur, dacc, dx,
     yb, lob, dhb, igb, gsb, sx, sc, sz, sy, gsout,
     g0, g1, g2, g3,
@@ -133,11 +134,13 @@
         greet({"s": 1 - s, "yh": c, "c": yh})
         pl.semaphore_wait(barrier, 12)
 
-    own_rows = pl.ds(pl.multiple_of((2 * x + c) * BLK, BLK), BLK)
+    def rows_of(xi, h, ci):
+        return pl.ds(pl.multiple_of(xi * 128 + h * BLK + ci * HALF, HALF), HALF)
+
     mirror = {"yh": c, "c": yh}
-    mirror_rows = pl.ds(pl.multiple_of((2 * x + yh) * BLK, BLK), BLK)
     swaps = (
-        (inp.at[s], hbuf.at[0, mirror_rows]),
+        (inp.at[s, pl.ds(0, HALF)], hbuf.at[0, rows_of(x, 0, yh)]),
+        (inp.at[s, pl.ds(HALF, HALF)], hbuf.at[0, rows_of(x, 1, yh)]),
         (seg.at[s], segb),
         (cot.at[s], cotb),
     )
@@ -218,101 +221,135 @@
             wl_copy(k).start()
 
     swap_start(0)
+    swap_start(1)
     spread(4)
     spread(QKV)
-    swap_start(1)
+    swap_start(2)
     spread(OUT)
     spread(UP)
     spread(DOWN)
-    swap_start(2)
+    swap_start(3)
 
     def arrival(i):
         return i + (i // 2) * (5 - 2 * i)
 
-    def ag_direct(ph, view, d):
-        block = view.at[own_rows]
-        return remote(block, block, ag_s.at[ph, d], ag_r.at[ph, d], {"x": lax.rem(x + d, 4)})
-
-    def ag_forward(ph, view, d):
-        rows = pl.ds(pl.multiple_of((2 * lax.rem(x + 4 - d, 4) + c) * BLK, BLK), BLK)
-        block = view.at[rows]
-        return remote(block, block, cg_s.at[ph, d], cg_r.at[ph, d], core)
-
-    def ag_start(ph, view):
+    def reversed_arrival(i):
+        return arrival(3 - i)
+
+    def ag_direct(ph, view, h, d):
+        block = view.at[rows_of(x, h, c)]
+        sem = 4 * h + d
+        return remote(block, block, ag_s.at[ph, sem], ag_r.at[ph, sem], {"x": lax.rem(x + d, 4)})
+
+    def ag_forward(ph, view, h, d):
+        block = view.at[rows_of(lax.rem(x + 4 - d, 4), h, c)]
+        return remote(block, block, cg_s.at[ph, 4 * h + d], cg_r.at[ph, 4 * h + d], core)
+
+    def ag_start(ph, view, h):
         for d in (1, 3, 2):
-            ag_direct(ph, view, d).start()
-        ag_forward(ph, view, 0).start()
-
-    def ag_block(ph, view, i):
-        d = arrival(i)
-
-        @pl.when(i > 0)
-        def _():
-            ag_direct(ph, view, d).wait_recv()
-            ag_forward(ph, view, d).start()
-
-        ag_forward(ph, view, d).wait_recv()
-        return pl.multiple_of(lax.rem(x + 4 - d, 4) * 128, 128)
+            ag_direct(ph, view, h, d).start()
+        ag_forward(ph, view, h, 0).start()
+
+    def block_rows(h, d):
+        return pl.ds(pl.multiple_of(lax.rem(x + 4 - d, 4) * 128 + h * BLK, BLK), BLK)
+
+    def pair_rows(t, order):
+        h = t // 2
+        i = 2 * (t - 2 * h)
+        return block_rows(h, order(i)), block_rows(h, order(i + 1))
+
+    def load(ref, lead, pair):
+        return jnp.concatenate([ref[(*lead, at, slice(None))] for at in pair], axis=0)
+
+    def store(ref, lead, pair, value):
+        for i, at in enumerate(pair):
+            ref[(*lead, at, slice(None))] = value[i * BLK : (i + 1) * BLK]
+
+    def ag_pair(ph, view, t):
+        h = t // 2
+
+        @pl.when(t == 2 * h)
+        def _():
+            for d in (1, 3):
+                ag_direct(ph, view, h, d).wait_recv()
+                ag_forward(ph, view, h, d).start()
+
+        @pl.when(t != 2 * h)
+        def _():
+            ag_direct(ph, view, h, 2).wait_recv()
+            ag_forward(ph, view, h, 2).start()
+
+        i = 2 * (t - 2 * h)
+        ag_forward(ph, view, h, arrival(i)).wait_recv()
+        ag_forward(ph, view, h, arrival(i + 1)).wait_recv()
+        return pair_rows(t, arrival)
 
     def ag_end(ph, view):
+        for h in range(2):
+            for d in (1, 2, 3):
+                ag_direct(ph, view, h, d).wait_send()
+            for d in range(4):
+                ag_forward(ph, view, h, d).wait_send()
+
+    my_half = pl.ds(pl.multiple_of(c * HALF, HALF), HALF)
+    other_half = pl.ds(pl.multiple_of((1 - c) * HALF, HALF), HALF)
+
+    def ra_copy(ph, slot):
+        return remote(aout.at[slot], ain.at[ph, slot], ra_s.at[ph, slot], ra_r.at[ph, slot], core)
+
+    def rb_copy(ph, slot):
+        target = {"x": lax.rem(x + 8 - slot, 4)}
+        return remote(bout.at[slot], bin_.at[ph, slot], rb_s.at[ph, slot], rb_r.at[ph, slot], target)
+
+    def rs_begin(ph, slot, value):
+        part[slot] = value
+        aout[slot] = part[slot, other_half, :].astype(BF)
+        ra_copy(ph, slot).start()
+
+    def rs_pass(ph, h, d):
+        slot = 4 * h + d
+        ra_copy(ph, slot).wait_recv()
+        total = part[slot, my_half, :] + ain[ph, slot].astype(F32)
+
+        @pl.when(d == 0)
+        def _():
+            res[h] = total
+
+        @pl.when(d != 0)
+        def _():
+            bout[slot] = total.astype(BF)
+            rb_copy(ph, slot).start()
+
+    def rs_loop(ph, order, step):
+        def one(t, carry):
+            @pl.when(t < 4)
+            def _():
+                h = t // 2
+                value = step(t)
+                for i in range(2):
+                    d = order(2 * (t - 2 * h) + i)
+                    rs_begin(ph, 4 * h + d, value[i * BLK : (i + 1) * BLK])
+
+            @pl.when(t > 0)
+            def _():
+                h = (t - 1) // 2
+                for i in range(2):
+                    rs_pass(ph, h, order(2 * (t - 1 - 2 * h) + i))
+
+            return carry
+
+        lax.fori_loop(0, 5, one, 0)
+
+    def rs_end(ph, h):
+        total = res[h]
+        for d in (1, 3, 2):
+            slot = 4 * h + d
+            rb_copy(ph, slot).wait_recv()
+            total = total + bin_[ph, slot].astype(F32)
+        for d in range(4):
+            ra_copy(ph, 4 * h + d).wait_send()
         for d in (1, 2, 3):
-            ag_direct(ph, view, d).wait_send()
-        for d in range(4):
-            ag_forward(ph, view, d).wait_send()
-
-    mine64 = pl.ds(pl.multiple_of(c * BLK, BLK), BLK)
-    theirs64 = pl.ds(pl.multiple_of((1 - c) * BLK, BLK), BLK)
-
-    def ra_copy(ph, d):
-        return remote(aout.at[d], ain.at[ph, d], ra_s.at[ph, d], ra_r.at[ph, d], core)
-
-    def rb_copy(ph, d):
-        return remote(
-            bout.at[d], bin_.at[ph, d], rb_s.at[ph, d], rb_r.at[ph, d], {"x": lax.rem(x + 4 - d, 4)}
-        )
-
-    def rs_begin(ph, d, value):
-        part[d] = value
-        aout[d] = part[d, theirs64, :].astype(BF)
-        ra_copy(ph, d).start()
-
-    def rs_pass(ph, d):
-        ra_copy(ph, d).wait_recv()
-        total = part[d, mine64, :] + ain[ph, d].astype(F32)
-
-        @pl.when(d == 0)
-        def _():
-            res[...] = total
-
-        @pl.when(d != 0)
-        def _():
-            bout[d] = total.astype(BF)
-            rb_copy(ph, d).start()
-
-    def rs_loop(ph, order, step):
-        def one(i, carry):
-            @pl.when(i < 4)
-            def _():
-                d = order(i)
-                rs_begin(ph, d, step(i, d))
-
-            @pl.when(i > 0)
-            def _():
-                rs_pass(ph, order(i - 1))
-
-            return carry
-
-        lax.fori_loop(0, 5, one, 0)
-
-    def rs_end(ph):
-        total = res[...]
-        for d in (1, 3, 2):
-            rb_copy(ph, d).wait_recv()
-            total = total + bin_[ph, d].astype(F32)
-        for d in range(4):
-            ra_copy(ph, d).wait_send()
-        for d in (1, 2, 3):
-            rb_copy(ph, d).wait_send()
+            rb_copy(ph, 4 * h + d).wait_send()
         return total
 
     lanes = lax.broadcasted_iota(jnp.int32, (1, 128), 1) < 64
@@ -341,11 +378,9 @@
                 home_copy(l, src, dst, send, recv).wait_send()
                 remote(src.at[l], dst.at[l], send.at[l], recv.at[l], core).wait_recv()
 
-    def reversed_arrival(i):
-        return arrival(3 - i)
-
-    swap_wait(0)
-    ag_start(FA, hbuf.at[0])
+    for h in range(2):
+        swap_wait(h)
+        ag_start(FA, hbuf.at[0], h)
     relay(0, 4)
     relay(0, QKV)
     relay(1, 4)
@@ -354,9 +389,13 @@
     def _():
         wl_copy(4).wait()
 
-    swap_wait(1)
+    swap_wait(2)
     documents = lax.broadcasted_iota(jnp.int32, (8, SEQ), 0) == segb[...]
     documents = documents.astype(F32).astype(BF)
+    put = lax.broadcasted_iota(jnp.int32, (SEQ, SEQ), 1)
+    put = put - lax.rem(put, 128) + lax.rem(put, 64) // 32 * 64 + lax.rem(put, 128) // 64 * 32 + lax.rem(put, 32)
+    move = lax.broadcasted_iota(jnp.int32, (SEQ, SEQ), 0) == put
+    documents = dot_nn(documents, move.astype(F32).astype(BF)).astype(BF)
     bias[...] = jnp.where(dot_tn(documents, documents) > 0.5, 0.0, -1e30)
 
     def forward(l, carry):
@@ -364,22 +403,17 @@
         out_b, gain_a, shift_a = small[0:1], small[1:2], small[2:3]
         down_b, gain_b, shift_b = small[3:4], small[4:5], small[5:6]
         view = hbuf.at[l]
-
-        @pl.when(l == 1)
-        def _():
-            ag_start(FA, view)
-
         ready(l, QKV)
 
-        def project(i, carry):
-            r0 = ag_block(FA, view, i)
-            rows = hbuf[l, pl.ds(r0, 128), :]
+        def project(t, carry):
+            at = ag_pair(FA, view, t)
+            rows = load(hbuf, (l,), at)
             q = dot_nn(rows, wq[l, 0]) + sw[l, 6:7, 512:640]
             k = dot_nn(rows, wq[l, 1])
             v = dot_nn(rows, wq[l, 2]) + sw[l, 6:7, 640:768]
-            qkv[l, 0, pl.ds(r0, 128), :] = q.astype(BF)
-            qkv[l, 1, pl.ds(r0, 128), :] = k.astype(BF)
-            qkv[l, 2, pl.ds(r0, 128), :] = v.astype(BF)
+            store(qkv, (l, 0), at, q.astype(BF))
+            store(qkv, (l, 1), at, k.astype(BF))
+            store(qkv, (l, 2), at, v.astype(BF))
             return carry
 
         lax.fori_loop(0, 4, project, 0)
@@ -391,20 +425,21 @@
 
         ready(l, OUT)
 
-        def attend(i, d):
-            r0 = pl.multiple_of(lax.rem(x + 4 - d, 4) * 128, 128)
-            q = qkv[l, 0, pl.ds(r0, 128), :]
+        def attend(t):
+            at = pair_rows(t, reversed_arrival)
+            q = load(qkv, (l, 0), at)
+            mask = load(bias, (), at)
             keys = qkv[l, 1]
             values = qkv[l, 2]
             heads = []
-            for h in range(2):
-                scores = dot_nt(q * head_mask[h], keys) * 0.125 + bias[pl.ds(r0, 128), :]
+            for j in range(2):
+                scores = dot_nt(q * head_mask[j], keys) * 0.125 + mask
                 e = jnp.exp(scores - jnp.max(scores, axis=-1, keepdims=True))
                 p = (e * (1.0 / jnp.sum(e, axis=-1, keepdims=True))).astype(BF)
-                probs[l, h, pl.ds(r0, 128), :] = p
+                store(probs, (l, j), at, p)
                 heads.append(dot_nn(p, values))
             block = jnp.where(first_head, heads[0], heads[1]).astype(BF)
-            att[l, pl.ds(r0, 128), :] = block
+            store(att, (l,), at, block)
             return dot_nn(block, wo[l])
 
         rs_loop(FA, reversed_arrival, attend)
@@ -415,41 +450,44 @@
             for k in (QKV, OUT, UP, DOWN):
                 relay(1, k)
 
-        r1 = hbuf[l, own_rows, :].astype(F32) + rs_end(FA) + out_b
+        ar_view = arbuf.at[l]
+        for h in range(2):
+            r1 = hbuf[l, rows_of(x, h, c), :].astype(F32) + rs_end(FA, h) + out_b
+            n, scale = normed(r1)
+            n1[l, h] = n
+            sc1[l, h] = jnp.broadcast_to(scale, (HALF, 128))
+            a = n * gain_a + shift_a
+            abuf[h] = a
+            arbuf[l, rows_of(x, h, c), :] = a.astype(BF)
+            ag_start(FM, ar_view, h)
         ag_end(FA, view)
-        n, scale = normed(r1)
-        n1[l] = n
-        sc1[l] = jnp.broadcast_to(scale, (BLK, 128))
-        a = n * gain_a + shift_a
-        abuf[...] = a
-        arbuf[l, own_rows, :] = a.astype(BF)
-        ar_view = arbuf.at[l]
-        ag_start(FM, ar_view)
         ready(l, UP)
         ready(l, DOWN)
 
-        def feed(i, d):
-            r0 = ag_block(FM, ar_view, i)
-            u = dot_nn(arbuf[l, pl.ds(r0, 128), :], wu[l]) + sw[l, 6:7, 0:512]
+        def feed(t):
+            at = ag_pair(FM, ar_view, t)
+            u = dot_nn(load(arbuf, (l,), at), wu[l]) + sw[l, 6:7, 0:512]
             cdf = 0.5 * (1.0 + lax.erf(u * 0.7071067811865476))
-            gp[l, pl.ds(r0, 128), :] = cdf + u * (jnp.exp(-0.5 * u * u) * 0.3989422804014327)
+            store(gp, (l,), at, cdf + u * (jnp.exp(-0.5 * u * u) * 0.3989422804014327))
             g = (u * cdf).astype(BF)
-            gr[l, pl.ds(r0, 128), :] = g
+            store(gr, (l,), at, g)
             return dot_nn(g, wd[l])
 
         rs_loop(FM, arrival, feed)
-        r2 = abuf[...] + rs_end(FM) + down_b
+        for h in range(2):
+            r2 = abuf[h] + rs_end(FM, h) + down_b
+            n, scale = normed(r2)
+            n2[l, h] = n
+            sc2[l, h] = jnp.broadcast_to(scale, (HALF, 128))
+            y = (n * gain_b + shift_b).astype(BF)
+            yb[l, h * HALF : (h + 1) * HALF, :] = y
+
+            @pl.when(l == 0)
+            def _():
+                hbuf[1, rows_of(x, h, c), :] = y
+                ag_start(FA, hbuf.at[1], h)
+
         ag_end(FM, ar_view)
-        n, scale = normed(r2)
-        n2[l] = n
-        sc2[l] = jnp.broadcast_to(scale, (BLK, 128))
-        y = (n * gain_b + shift_b).astype(BF)
-        yb[l] = y
-
-        @pl.when(l == 0)
-        def _():
-            hbuf[1, own_rows, :] = y
-
         home_start(l, yb, lob, lo_s, lo_r)
         return carry
 
@@ -568,98 +606,135 @@
         def _():
             gsout[6:7, :] = gsout[7:8, :]
 
-    swap_wait(2)
+    swap_wait(3)
+
+    def input_grad(l, h):
+        low = (abuf[h] + rs_end(BA, h)).astype(BF)
+        dhb[l, h * HALF : (h + 1) * HALF, :] = low
+        return low.astype(F32)
+
+    def grads_qkv(l):
+        def some(i, carry):
+            cols = pl.ds(pl.multiple_of(i * 128, 128), 128)
+            rows = hbuf[l, :, cols]
+            for j in range(3):
+                g0[l, j, cols, :] = dot_tn(rows, dx[j]).astype(BF)
+            return carry
+
+        lax.fori_loop(0, 8, some, 0)
+        gz_start(l, QKV)
+
+    def grads_out(l):
+        g1[l] = dot_tn(att[l], dprbuf[...]).astype(BF)
+        gz_start(l, OUT)
+
+    def grads_down(l):
+        def some(i, carry):
+            cols = pl.ds(pl.multiple_of(i * 128, 128), 128)
+            g3[l, cols, :] = dot_tn(gr[l, :, cols], dmbuf[...]).astype(BF)
+            return carry
+
+        lax.fori_loop(0, 4, some, 0)
+        gz_start(l, DOWN)
+
+    def grads_up(l):
+        def some(i, carry):
+            cols = pl.ds(pl.multiple_of(i * 128, 128), 128)
+            g2[l, cols, :] = dot_tn(arbuf[l, :, cols], dur[...]).astype(BF)
+            return carry
+
+        lax.fori_loop(0, 8, some, 0)
+        gz_start(l, UP)
 
     def backward(step_index, carry):
         l = 1 - step_index
         small = sw[l]
         gain_a, gain_b = small[1:2], small[4:5]
-
-        @pl.when(l == 1)
-        def _():
-            res[...] = cotb[...].astype(F32)
-
-        @pl.when(l == 0)
-        def _():
-            res[...] = dhb[1].astype(F32)
-
-        dy = res[...]
-        n = n2[l]
-        dr2 = norm_back(dy, gain_b, n, sc2[l, :, 0:1])
-        dmbuf[own_rows, :] = dr2.astype(BF)
-        ag_start(BM, dmbuf)
         gsb[l] = jnp.zeros((8, D), F32)
-        gsb[l, 4:5, :] = col_sum(dy * n)
-        gsb[l, 5:6, :] = col_sum(dy)
-        gsb[l, 3:4, :] = col_sum(dr2)
-        abuf[...] = dr2
-
-        def feed_back(i, d):
-            r0 = ag_block(BM, dmbuf, i)
-            dg = dot_nt(dmbuf[pl.ds(r0, 128), :], wd[l])
-            du = dg * gp[l, pl.ds(r0, 128), :]
+        for h in range(2):
+            @pl.when(l == 1)
+            def _():
+                dyb[...] = cotb[h * HALF : (h + 1) * HALF, :].astype(F32)
+
+            @pl.when(l == 0)
+            def _():
+                dyb[...] = input_grad(1, h)
+
+            dy = dyb[...]
+            n = n2[l, h]
+            dr2 = norm_back(dy, gain_b, n, sc2[l, h, :, 0:1])
+            dmbuf[rows_of(x, h, c), :] = dr2.astype(BF)
+            ag_start(BM, dmbuf, h)
+            abuf[h] = dr2
+            gsb[l, 4:5, :] += col_sum(dy * n)
+            gsb[l, 5:6, :] += col_sum(dy)
+            gsb[l, 3:4, :] += col_sum(dr2)
+
+            @pl.when(l == 0)
+            def _():
+                if h == 0:
+                    grads_qkv(1)
+                else:
+                    grads_out(1)
+                    small_z(1)
+                    ag_end(BA, dprbuf)
+                    home_start(1, dhb, igb, ig_s, ig_r)
+
+        def feed_back(t):
+            at = ag_pair(BM, dmbuf, t)
+            dg = dot_nt(load(dmbuf, (), at), wd[l])
+            du = dg * load(gp, (l,), at)
             gsb[l, 6:7, 0:512] += col_sum(du)
             low = du.astype(BF)
-            dur[pl.ds(r0, 128), :] = low
+            store(dur, (), at, low)
             return dot_nt(low, wu[l])
 
         rs_loop(BM, arrival, feed_back)
-
-        def grad_down(i, carry):
-            cols = pl.ds(pl.multiple_of(i * 128, 128), 128)
-            g3[l, cols, :] = dot_tn(gr[l, :, cols], dmbuf[...]).astype(BF)
-            return carry
-
-        lax.fori_loop(0, 4, grad_down, 0)
-        gz_start(l, DOWN)
-
-        def grad_up(i, carry):
-            cols = pl.ds(pl.multiple_of(i * 128, 128), 128)
-            g2[l, cols, :] = dot_tn(arbuf[l, :, cols], dur[...]).astype(BF)
-            return carry
-
-        lax.fori_loop(0, 8, grad_up, 0)
-        gz_start(l, UP)
-        da = abuf[...] + rs_end(BM)
+        for h in range(2):
+            da = abuf[h] + rs_end(BM, h)
+            n = n1[l, h]
+            dr1 = norm_back(da, gain_a, n, sc1[l, h, :, 0:1])
+            dprbuf[rows_of(x, h, c), :] = dr1.astype(BF)
+            ag_start(BA, dprbuf, h)
+            abuf[h] = dr1
+            gsb[l, 1:2, :] += col_sum(da * n)
+            gsb[l, 2:3, :] += col_sum(da)
+            gsb[l, 0:1, :] += col_sum(dr1)
+            if h == 0:
+                grads_down(l)
+            else:
+                grads_up(l)
         ag_end(BM, dmbuf)
-        n = n1[l]
-        dr1 = norm_back(da, gain_a, n, sc1[l, :, 0:1])
-        dprbuf[own_rows, :] = dr1.astype(BF)
-        ag_start(BA, dprbuf)
-        gsb[l, 1:2, :] = col_sum(da * n)
-        gsb[l, 2:3, :] = col_sum(da)
-        gsb[l, 0:1, :] = col_sum(dr1)
-        abuf[...] = dr1
         dacc[...] = jnp.zeros_like(dacc)
 
         @pl.when(l == 0)
         def _():
+            small_y(1)
             for k in (DOWN, UP):
                 gy_start(1, k)
 
-        def attend_back(i, carry):
-            r0 = ag_block(BA, dprbuf, i)
-            rows = pl.ds(r0, 128)
-            grad = dot_nt(dprbuf[rows, :], wo[l]).astype(BF)
-            q = qkv[l, 0, rows, :]
+        def attend_back(t, carry):
+            at = ag_pair(BA, dprbuf, t)
+            grad = dot_nt(load(dprbuf, (), at), wo[l]).astype(BF)
+            q = load(qkv, (l, 0), at)
             keys = qkv[l, 1]
             values = qkv[l, 2]
             heads = []
             dk = dacc[0]
             dv = dacc[1]
-            for h in range(2):
-                own = grad * head_mask[h]
-                low_p = probs[l, h, rows, :]
+            for j in range(2):
+                own = grad * head_mask[j]
+                low_p = load(probs, (l, j), at)
                 p = low_p.astype(F32)
                 dp = dot_nt(own, values)
                 ds = (p * (dp - jnp.sum(p * dp, axis=-1, keepdims=True))).astype(BF)
                 heads.append(dot_nn(ds, keys))
-                dk = dk + dot_tn(ds, q * head_mask[h])
+                dk = dk + dot_tn(ds, q * head_mask[j])
                 dv = dv + dot_tn(low_p, own)
             dacc[0] = dk
             dacc[1] = dv
             dq = (jnp.where(first_head, heads[0], heads[1]) * 0.125).astype(BF)
-            dx[0, rows, :] = dq
+            store(dx, (0,), at, dq)
             gsb[l, 6:7, 512:640] += col_sum(dq.astype(F32))
             return carry
 
@@ -670,37 +745,27 @@
         gsb[l, 6:7, 640:768] = col_sum(dv.astype(F32))
         small_x(l)
 
-        def input_back(i, d):
-            rows = pl.ds(pl.multiple_of(lax.rem(x + 4 - d, 4) * 128, 128), 128)
+        def input_back(t):
+            at = pair_rows(t, reversed_arrival)
             return (
-                dot_nt(dx[0, rows, :], wq[l, 0])
-                + dot_nt(dx[1, rows, :], wq[l, 1])
-                + dot_nt(dx[2, rows, :], wq[l, 2])
+                dot_nt(load(dx, (0,), at), wq[l, 0])
+                + dot_nt(load(dx, (1,), at), wq[l, 1])
+                + dot_nt(load(dx, (2,), at), wq[l, 2])
             )
 
         rs_loop(BA, reversed_arrival, input_back)
         small_core(l)
-
-        def grad_qkv(i, carry):
-            cols = pl.ds(pl.multiple_of(i * 128, 128), 128)
-            rows = hbuf[l, :, cols]
-            for j in range(3):
-                g0[l, j, cols, :] = dot_tn(rows, dx[j]).astype(BF)
-            return carry
-
-        lax.fori_loop(0, 8, grad_qkv, 0)
-        gz_start(l, QKV)
-        g1[l] = dot_tn(att[l], dprbuf[...]).astype(BF)
-        gz_start(l, OUT)
-        small_z(l)
-        dh = (abuf[...] + rs_end(BA)).astype(BF)
-        ag_end(BA, dprbuf)
-        dhb[l] = dh
-        home_start(l, dhb, igb, ig_s, ig_r)
-        small_y(l)
         return carry
 
     lax.fori_loop(0, 2, backward, 0)
+    grads_qkv(0)
+    grads_out(0)
+    small_z(0)
+    for h in range(2):
+        input_grad(0, h)
+    ag_end(BA, dprbuf)
+    home_start(0, dhb, igb, ig_s, ig_r)
+    small_y(0)
 
     for k in (QKV, OUT):
         gy_start(1, k)
@@ -778,19 +843,20 @@
     scratch += [vm((2, *shape), BF) for shape in WSHAPES]
     scratch += [vm((2, 8, D), F32)]
     scratch += [vm((2, SEQ, D), BF)] * 2 + [vm((SEQ, D), BF)] * 2
-    scratch += [vm((4, 4, BLK, D), BF)] * 2 + [vm((4, BLK, D), BF)] * 2 + [vm((4, 128, D), F32)]
+    scratch += [vm((4, 8, HALF, D), BF)] * 2 + [vm((8, HALF, D), BF)] * 2 + [vm((8, BLK, D), F32)]
     scratch += [
         vm((2, 3, SEQ, 128), BF),
         vm((2, SEQ, 128), BF),
         vm((2, 2, SEQ, SEQ), BF),
         vm((2, SEQ, FFS), F32),
         vm((2, SEQ, FFS), BF),
-        vm((2, BLK, D), F32),
-        vm((2, BLK, D), F32),
-        vm((2, BLK, 128), F32),
-        vm((2, BLK, 128), F32),
-        vm((BLK, D), F32),
-        vm((BLK, D), F32),
+        vm((2, 2, HALF, D), F32),
+        vm((2, 2, HALF, D), F32),
+        vm((2, 2, HALF, 128), F32),
+        vm((2, 2, HALF, 128), F32),
+        vm((2, HALF, D), F32),
+        vm((2, HALF, D), F32),
+        vm((HALF, D), F32),
     ]
     scratch += [
         vm((8, SEQ), jnp.int32),
@@ -808,8 +874,8 @@
     scratch += [vm((3, *shape), BF) for shape in PSHAPES]
     scratch += [vm(shape, BF) for shape in WSHAPES]
     dma = pltpu.SemaphoreType.DMA
-    scratch += [dma((3,)), dma((3,)), dma((5, 4)), dma((2, 5)), dma((2, 4, 4)), dma((2, 4, 4)), dma((5,))]
-    scratch += [dma((4, 4))] * 8
+    scratch += [dma((4,)), dma((4,)), dma((5, 4)), dma((2, 5)), dma((2, 4, 4)), dma((2, 4, 4)), dma((5,))]
+    scratch += [dma((4, 8))] * 8
     scratch += [dma((2,))] * 4
     scratch += [dma((2, 4, 4)), dma((2, 4, 4)), dma((2, 4)), dma((4, 4))]
     scratch += [dma((4, 4))] * 4 + [dma((7,))]
@@ -833,31 +899,58 @@
     )(*operands)
 
 
+def finish_kernel(lo, ig, gq, go, gu, gd, gs, lo_o, ig_o, gq_o, qv_o, go_o, ob_o, ga_o, sa_o, gu_o, ub_o, gd_o, db_o, gb_o, sb_o):
+    lo_o[0, :, 0] = lo[...]
+    ig_o[0, :, 0] = ig[...]
+    gq_o[0] = gq[...].astype(F32)
+    go_o[0] = go[...].astype(F32)
+    gu_o[0] = gu[...].astype(F32)
+    gd_o[0] = gd[...].astype(F32)
+    for row, ref in enumerate((ob_o, ga_o, sa_o, db_o, gb_o, sb_o)):
+        ref[...] = gs[row : row + 1, :]
+    ub_o[...] = gs[6:7, 0:512]
+    qv_o[0, 0:1, :] = gs[6:7, 512:640]
+    qv_o[0, 1:2, :] = gs[6:7, 640:768]
+
+
+def finish(lo, ig, *rest):
+    steps = 4
+    row = ((1, D), lambda i: (0, 0))
+    wide = ((2, BLK // steps, D), lambda i: (0, i, 0))
+    wide_out = ((1, 2, 1, BLK // steps, D), lambda i: (0, 0, 0, i, 0))
+    wmaps = ((lambda i: (0, i, 0)), (lambda i: (i, 0)), (lambda i: (i, 0)), (lambda i: (i, 0)))
+    omaps = ((lambda i: (0, 0, i, 0)),) + ((lambda i: (0, i, 0)),) * 3
+    gq_o, go_o, gu_o, gd_o = (((1, *shape), m) for shape, m in zip(PSHAPES, omaps))
+    specs_in = [wide, wide, *zip(PSHAPES, wmaps), ((8, D), lambda i: (0, 0))]
+    specs_out = [
+        wide_out, wide_out, gq_o, ((1, 2, 128), lambda i: (0, 0, 0)), go_o, row, row, row,
+        gu_o, ((1, FFS), lambda i: (0, 0)), gd_o, row, row, row,
+    ]
+    full = [
+        ((1, 2, 1, BLK, D), BF), ((1, 2, 1, BLK, D), BF), ((1, 3, D, 128), F32), ((1, 2, 128), F32),
+        ((1, 128, D), F32), ((1, D), F32), ((1, D), F32), ((1, D), F32), ((1, D, FFS), F32),
+        ((1, FFS), F32), ((1, FFS, D), F32), ((1, D), F32), ((1, D), F32), ((1, D), F32),
+    ]
+    return pl.pallas_call(
+        finish_kernel,
+        grid=(steps,),
+        out_shape=[jax.ShapeDtypeStruct(*leaf) for leaf in full],
+        in_specs=[pl.BlockSpec(*spec) for spec in specs_in],
+        out_specs=[pl.BlockSpec(*spec) for spec in specs_out],
+        compiler_params=pltpu.CompilerParams(vmem_limit_bytes=60 * 1024 * 1024),
+    )(lo, ig, *rest)
+
+
 def local(
     inputs, segments, qkv_weight, qv_bias, out_weight, out_bias, gain_one, shift_one,
     up_weight, up_bias, down_weight, down_bias, gain_two, shift_two, cotangent,
 ):
-    lo, ig, gq, go, gu, gd, gs = run(
+    results = run(
         inputs[:, 0], cotangent[:, 0], segments,
         qkv_weight[0], out_weight[0], up_weight[0], down_weight[0],
         out_bias, gain_one, shift_one, down_bias, gain_two, shift_two, up_bias, qv_bias,
     )
-    return (
-        lo[None, :, None],
-        ig[None, :, None],
-        gq[None].astype(F32),
-        gs[6, 512:768].reshape(1, 2, 128),
-        go[None].astype(F32),
-        gs[0:1],
-        gs[1:2],
-        gs[2:3],
-        gu[None].astype(F32),
-        gs[6:7, 0:512],
-        gd[None].astype(F32),
-        gs[3:4],
-        gs[4:5],
-        gs[5:6],
-    )
+    return tuple(finish(*results))
 
 
 def solution(mesh):

time: 283 us -> 251 us (0.89)
  Pallas kernels: 270 us -> 250 us
  other arithmetic: 6.49 us -> 0 us
  local copies, waits for them, and re-layouts: 5.69 us -> 0 us
    pallas_call x1, Pallas kernels: 270 us -> 244 us  [run(): pl.pallas_call(kernel, out_shape=[jax.ShapeDtypeStruct((2, BLK, D), BF),...]
    convert_element_type x4 -> x0, other arithmetic: 6.49 us -> none  [the longest x1 2.79 us: local(): gd[None].astype(F32)]
    pallas_call x0 -> x1, Pallas kernels: none -> 5.42 us  [finish(): pl.pallas_call(finish_kernel, grid=(steps,), out_shape=[jax.ShapeDtypeStr...]
    slice x3 -> x0, local copies, waits for them, and re-layouts: 4.26 us -> none  [the longest x1 1.71 us: local(): gs[5:6]]
where the time goes in v3:
time: 251 us; the launch traced here: 250 us
  Pallas kernels  250 us (100%)
    pallas_call x1, Pallas kernels, run(): pl.pallas_call(kernel, out_shape=[jax.ShapeDtypeStruct((2, BLK, D), BF),...  244 us
    pallas_call x1, Pallas kernels, finish(): pl.pallas_call(finish_kernel, grid=(steps,), out_shape=[jax.ShapeDtypeStr...  5.42 us

profile of v3, /device:TPU:1, one launch (start us, length us, event | category | flops | bytes accessed | tf_op | source)
XLA Modules:
  0.0 250.5 jit_solution(12754051910655106231)
XLA Ops:
  0.7 244.4 %shard_map.254 = (bf16[2,64,1024]{2,1,0:T(8,128)(2,1)}, bf16[2,64,1024]{2,1,0:T(8,128)(2,1)}, bf16[3,1024,128]{2,1,0:T(8,128)(2,1)}, bf16[128,1024]{1,0:T(8,128)...) custom-call(bf16[2,64,1024]{2,1,0:T(8,128)(2,1)} %bitcast.9, ...), custom_call_target="tpu_custom_call" | custom-call | tf_op jit(solution)/shard_map/pallas_call | solution.py:885
  245.0 5.4 %shard_map.255 = (bf16[1,2,1,64,1024]{4,3,2,1,0:T(8,128)(2,1)}, bf16[1,2,1,64,1024]{4,3,2,1,0:T(8,128)(2,1)}, f32[1,3,1024,128]{3,2,1,0:T(8,128)}, f32[1,2,128]{...) custom-call(bf16[2,64,1024]{2,1,0:T(8,128)(2,1)} %get-tuple-element., ...), custom_call_target="tpu_custom_call" | custom-call | tf_op jit(solution)/shard_map/pallas_call | solution.py:934

commit v4 on v3

--- a/solution.py
+++ b/solution.py
@@ -167,17 +167,19 @@
         def _():
             remote(src, dst, swap_s.at[i], swap_r.at[i], mirror).wait()
 
-    def wy_copy(k, i):
+    def wy_copy(k, i, j):
         if k == 4:
-            return remote(sw_in, sw.at[s], wy_s.at[k, i], wy_r.at[s, k], y_dev(i))
-        src = at_piece(weights_in[k], k, z)
-        return remote(src, at_piece(weights[k], k, z, (s,)), wy_s.at[k, i], wy_r.at[s, k], y_dev(i))
-
-    def wy_arrival(l, k):
+            return remote(sw_in, sw.at[s], wy_s.at[k, i, j], wy_r.at[s, k, j], y_dev(i))
+        zi = lax.rem(z + j, 4)
+        src = at_piece(weights_in[k], k, zi)
+        dst = at_piece(weights[k], k, zi, (s,))
+        return remote(src, dst, wy_s.at[k, i, j], wy_r.at[s, k, j], y_dev(i))
+
+    def wy_arrival(l, k, j):
         if k == 4:
-            return remote(sw_in, sw.at[l], wy_s.at[k, 0], wy_r.at[l, k], core)
-        dst = at_piece(weights[k], k, z, (l,))
-        return remote(dst, dst, wy_s.at[k, 0], wy_r.at[l, k], core)
+            return remote(sw_in, sw.at[l], wy_s.at[k, 0, j], wy_r.at[l, k, j], core)
+        dst = at_piece(weights[k], k, lax.rem(z + j, 4), (l,))
+        return remote(dst, dst, wy_s.at[k, 0, j], wy_r.at[l, k, j], core)
 
     def wl_copy(k):
         if k == 4:
@@ -185,11 +187,11 @@
         return pltpu.make_async_copy(weights_in[k], weights[k].at[s], wl.at[k])
 
     def wz_copy(l, k, d):
-        piece = at_piece(weights[k], k, z, (l,))
+        piece = at_piece(weights[k], k, lax.rem(z + d // 2, 4), (l,))
         return remote(piece, piece, wz_s.at[l, k, d], wz_r.at[l, k, d], z_dev(d))
 
     def wz_arrival(l, k, d):
-        piece = at_piece(weights[k], k, lax.rem(z + 4 - d, 4), (l,))
+        piece = at_piece(weights[k], k, lax.rem(z + (3 if d == 1 else 2), 4), (l,))
         return remote(piece, piece, wz_s.at[l, k, d], wz_r.at[l, k, d], z_dev(d))
 
     def mine(l):
@@ -198,10 +200,11 @@
     def relay(l, k):
         @pl.when(jnp.logical_not(mine(l)))
         def _():
-            wy_arrival(l, k).wait_recv()
+            wy_arrival(l, k, 0).wait_recv()
             if k != 4:
-                for d in (1, 3, 2):
-                    wz_copy(l, k, d).start()
+                wz_copy(l, k, 1).start()
+                wy_arrival(l, k, 1).wait_recv()
+                wz_copy(l, k, 3).start()
 
     def ready(l, k):
         @pl.when(mine(l))
@@ -210,25 +213,23 @@
 
         @pl.when(jnp.logical_not(mine(l)))
         def _():
-            for d in (1, 3, 2):
+            for d in (1, 3):
                 wz_arrival(l, k, d).wait_recv()
 
-    def spread(k):
-        @pl.when(diag)
-        def _():
-            for i in (1, 3, 2):
-                wy_copy(k, i).start()
+    def spread(l, k):
+        @pl.when(mine(l))
+        def _():
+            for j in range(1 if k == 4 else 2):
+                for i in (1, 3, 2):
+                    wy_copy(k, i, j).start()
             wl_copy(k).start()
 
     swap_start(0)
     swap_start(1)
-    spread(4)
-    spread(QKV)
+    spread(0, 4)
+    spread(0, QKV)
+    spread(1, 4)
     swap_start(2)
-    spread(OUT)
-    spread(UP)
-    spread(DOWN)
-    swap_start(3)
 
     def arrival(i):
         return i + (i // 2) * (5 - 2 * i)
@@ -321,24 +322,26 @@
             rb_copy(ph, slot).start()
 
     def rs_loop(ph, order, step):
+        def pass_pair(t):
+            h = t // 2
+            for i in range(2):
+                rs_pass(ph, h, order(2 * (t - 2 * h) + i))
+
         def one(t, carry):
-            @pl.when(t < 4)
-            def _():
-                h = t // 2
-                value = step(t)
-                for i in range(2):
-                    d = order(2 * (t - 2 * h) + i)
-                    rs_begin(ph, 4 * h + d, value[i * BLK : (i + 1) * BLK])
+            h = t // 2
+            value = step(t)
+            for i in range(2):
+                d = order(2 * (t - 2 * h) + i)
+                rs_begin(ph, 4 * h + d, value[i * BLK : (i + 1) * BLK])
 
             @pl.when(t > 0)
             def _():
-                h = (t - 1) // 2
-                for i in range(2):
-                    rs_pass(ph, h, order(2 * (t - 1 - 2 * h) + i))
+                pass_pair(t - 1)
 
             return carry
 
-        lax.fori_loop(0, 5, one, 0)
+        lax.fori_loop(0, 4, one, 0)
+        pass_pair(3)
 
     def rs_end(ph, h):
         total = res[h]
@@ -382,13 +385,6 @@
         swap_wait(h)
         ag_start(FA, hbuf.at[0], h)
     relay(0, 4)
-    relay(0, QKV)
-    relay(1, 4)
-
-    @pl.when(diag)
-    def _():
-        wl_copy(4).wait()
-
     swap_wait(2)
     documents = lax.broadcasted_iota(jnp.int32, (8, SEQ), 0) == segb[...]
     documents = documents.astype(F32).astype(BF)
@@ -397,6 +393,15 @@
     move = lax.broadcasted_iota(jnp.int32, (SEQ, SEQ), 0) == put
     documents = dot_nn(documents, move.astype(F32).astype(BF)).astype(BF)
     bias[...] = jnp.where(dot_tn(documents, documents) > 0.5, 0.0, -1e30)
+    relay(0, QKV)
+    spread(0, OUT)
+    spread(0, UP)
+    spread(0, DOWN)
+    relay(1, 4)
+
+    @pl.when(diag)
+    def _():
+        wl_copy(4).wait()
 
     def forward(l, carry):
         small = sw[l]
@@ -418,14 +423,28 @@
 
         lax.fori_loop(0, 4, project, 0)
 
+        @pl.when(l == 1)
+        def _():
+            relay(1, UP)
+            relay(1, DOWN)
+
+
         @pl.when(l == 0)
         def _():
             relay(0, OUT)
-            relay(0, UP)
 
         ready(l, OUT)
 
         def attend(t):
+            @pl.when(jnp.logical_and(l == 0, t == 1))
+            def _():
+                for k in (QKV, OUT, UP, DOWN):
+                    spread(1, k)
+
+            @pl.when(jnp.logical_and(l == 0, t == 2))
+            def _():
+                relay(0, UP)
+
             at = pair_rows(t, reversed_arrival)
             q = load(qkv, (l, 0), at)
             mask = load(bias, (), at)
@@ -447,8 +466,6 @@
         @pl.when(l == 0)
         def _():
             relay(0, DOWN)
-            for k in (QKV, OUT, UP, DOWN):
-                relay(1, k)
 
         ar_view = arbuf.at[l]
         for h in range(2):
@@ -465,6 +482,10 @@
         ready(l, DOWN)
 
         def feed(t):
+            @pl.when(jnp.logical_and(l == 0, t == 3))
+            def _():
+                relay(1, QKV)
+
             at = ag_pair(FM, ar_view, t)
             u = dot_nn(load(arbuf, (l,), at), wu[l]) + sw[l, 6:7, 0:512]
             cdf = 0.5 * (1.0 + lax.erf(u * 0.7071067811865476))
@@ -488,6 +509,12 @@
                 ag_start(FA, hbuf.at[1], h)
 
         ag_end(FM, ar_view)
+
+        @pl.when(l == 0)
+        def _():
+            relay(1, OUT)
+            swap_start(3)
+
         home_start(l, yb, lob, lo_s, lo_r)
         return carry
 
@@ -745,6 +772,13 @@
         gsb[l, 6:7, 640:768] = col_sum(dv.astype(F32))
         small_x(l)
 
+        @pl.when(l == 0)
+        def _():
+            grads_qkv(0)
+            grads_out(0)
+            for k in (QKV, OUT):
+                gy_start(1, k)
+
         def input_back(t):
             at = pair_rows(t, reversed_arrival)
             return (
@@ -758,8 +792,8 @@
         return carry
 
     lax.fori_loop(0, 2, backward, 0)
-    grads_qkv(0)
-    grads_out(0)
+    for k in (DOWN, UP):
+        gy_start(0, k)
     small_z(0)
     for h in range(2):
         input_grad(0, h)
@@ -767,10 +801,6 @@
     home_start(0, dhb, igb, ig_s, ig_r)
     small_y(0)
 
-    for k in (QKV, OUT):
-        gy_start(1, k)
-    for k in (DOWN, UP):
-        gy_start(0, k)
     for k in (DOWN, UP):
         fz_start(k)
     for k in (QKV, OUT):
@@ -799,13 +829,14 @@
     def _():
         for k in range(5):
             for i in (1, 2, 3):
-                wy_copy(k, i).wait_send()
+                for j in range(1 if k == 4 else 2):
+                    wy_copy(k, i, j).wait_send()
 
     for l in range(2):
         for k in range(4):
             @pl.when(jnp.logical_not(mine(l)))
             def _():
-                for d in (1, 2, 3):
+                for d in (1, 3):
                     wz_copy(l, k, d).wait_send()
                 gy_copy(l, k).wait_send()
 
@@ -874,7 +905,7 @@
     scratch += [vm((3, *shape), BF) for shape in PSHAPES]
     scratch += [vm(shape, BF) for shape in WSHAPES]
     dma = pltpu.SemaphoreType.DMA
-    scratch += [dma((4,)), dma((4,)), dma((5, 4)), dma((2, 5)), dma((2, 4, 4)), dma((2, 4, 4)), dma((5,))]
+    scratch += [dma((4,)), dma((4,)), dma((5, 4, 2)), dma((2, 5, 2)), dma((2, 4, 4)), dma((2, 4, 4)), dma((5,))]
     scratch += [dma((4, 8))] * 8
     scratch += [dma((2,))] * 4
     scratch += [dma((2, 4, 4)), dma((2, 4, 4)), dma((2, 4)), dma((4, 4))]
@@ -913,15 +944,18 @@
     qv_o[0, 1:2, :] = gs[6:7, 640:768]
 
 
+FSHAPES = ((3, 512, 128), (64, D), (512, FFS), (256, D))
+
+
 def finish(lo, ig, *rest):
-    steps = 4
+    steps = 2
     row = ((1, D), lambda i: (0, 0))
     wide = ((2, BLK // steps, D), lambda i: (0, i, 0))
     wide_out = ((1, 2, 1, BLK // steps, D), lambda i: (0, 0, 0, i, 0))
     wmaps = ((lambda i: (0, i, 0)), (lambda i: (i, 0)), (lambda i: (i, 0)), (lambda i: (i, 0)))
     omaps = ((lambda i: (0, 0, i, 0)),) + ((lambda i: (0, i, 0)),) * 3
-    gq_o, go_o, gu_o, gd_o = (((1, *shape), m) for shape, m in zip(PSHAPES, omaps))
-    specs_in = [wide, wide, *zip(PSHAPES, wmaps), ((8, D), lambda i: (0, 0))]
+    gq_o, go_o, gu_o, gd_o = (((1, *shape), m) for shape, m in zip(FSHAPES, omaps))
+    specs_in = [wide, wide, *zip(FSHAPES, wmaps), ((8, D), lambda i: (0, 0))]
     specs_out = [
         wide_out, wide_out, gq_o, ((1, 2, 128), lambda i: (0, 0, 0)), go_o, row, row, row,
         gu_o, ((1, FFS), lambda i: (0, 0)), gd_o, row, row, row,

time: 251 us -> 231 us (0.920)
  Pallas kernels: 250 us -> 230 us
    pallas_call x1, Pallas kernels: 244 us -> 225 us  [run(): pl.pallas_call(kernel, out_shape=[jax.ShapeDtypeStruct((2, BLK, D), BF),...]
where the time goes in v4:
time: 231 us
  Pallas kernels  230 us (100%)
    pallas_call x1, Pallas kernels, run(): pl.pallas_call(kernel, out_shape=[jax.ShapeDtypeStruct((2, BLK, D), BF),...  225 us
    pallas_call x1, Pallas kernels, finish(): pl.pallas_call(finish_kernel, grid=(steps,), out_shape=[jax.ShapeDtypeStr...  4.62 us

profile of v4, /device:TPU:1, one launch (start us, length us, event | category | flops | bytes accessed | tf_op | source)
XLA Modules:
  0.0 230.6 jit_solution(174598435399454228)
XLA Ops:
  0.7 225.3 %shard_map.254 = (bf16[2,64,1024]{2,1,0:T(8,128)(2,1)}, bf16[2,64,1024]{2,1,0:T(8,128)(2,1)}, bf16[3,1024,128]{2,1,0:T(8,128)(2,1)}, bf16[128,1024]{1,0:T(8,128)...) custom-call(bf16[2,64,1024]{2,1,0:T(8,128)(2,1)} %bitcast.9, ...), custom_call_target="tpu_custom_call" | custom-call | tf_op jit(solution)/shard_map/pallas_call | solution.py:916
  225.9 4.6 %shard_map.255 = (bf16[1,2,1,64,1024]{4,3,2,1,0:T(8,128)(2,1)}, bf16[1,2,1,64,1024]{4,3,2,1,0:T(8,128)(2,1)}, f32[1,3,1024,128]{3,2,1,0:T(8,128)}, f32[1,2,128]{...) custom-call(bf16[2,64,1024]{2,1,0:T(8,128)(2,1)} %get-tuple-element., ...), custom_call_target="tpu_custom_call" | custom-call | tf_op jit(solution)/shard_map/pallas_call | solution.py:968

commit v5 on v4

--- a/solution.py
+++ b/solution.py
@@ -291,6 +291,9 @@
                 ag_direct(ph, view, h, d).wait_send()
             for d in range(4):
                 ag_forward(ph, view, h, d).wait_send()
+                ra_copy(ph, 4 * h + d).wait_send()
+            for d in (1, 2, 3):
+                rb_copy(ph, 4 * h + d).wait_send()
 
     my_half = pl.ds(pl.multiple_of(c * HALF, HALF), HALF)
     other_half = pl.ds(pl.multiple_of((1 - c) * HALF, HALF), HALF)
@@ -349,10 +352,6 @@
             slot = 4 * h + d
             rb_copy(ph, slot).wait_recv()
             total = total + bin_[ph, slot].astype(F32)
-        for d in range(4):
-            ra_copy(ph, 4 * h + d).wait_send()
-        for d in (1, 2, 3):
-            rb_copy(ph, 4 * h + d).wait_send()
         return total
 
     lanes = lax.broadcasted_iota(jnp.int32, (1, 128), 1) < 64

time: 231 us -> 230 us (level)
  no operation moved by 1% of the time
where the time goes in v5:
time: 230 us
  Pallas kernels  229 us (100%)
    pallas_call x1, Pallas kernels, run(): pl.pallas_call(kernel, out_shape=[jax.ShapeDtypeStruct((2, BLK, D), BF),...  224 us
    pallas_call x1, Pallas kernels, finish(): pl.pallas_call(finish_kernel, grid=(steps,), out_shape=[jax.ShapeDtypeStr...  4.62 us

profile of v5, /device:TPU:1, one launch (start us, length us, event | category | flops | bytes accessed | tf_op | source)
XLA Modules:
  0.0 229.6 jit_solution(5398264465659186977)
XLA Ops:
  0.7 224.3 %shard_map.254 = (bf16[2,64,1024]{2,1,0:T(8,128)(2,1)}, bf16[2,64,1024]{2,1,0:T(8,128)(2,1)}, bf16[3,1024,128]{2,1,0:T(8,128)(2,1)}, bf16[128,1024]{1,0:T(8,128)...) custom-call(bf16[2,64,1024]{2,1,0:T(8,128)(2,1)} %bitcast.9, ...), custom_call_target="tpu_custom_call" | custom-call | tf_op jit(solution)/shard_map/pallas_call | solution.py:915
  225.0 4.6 %shard_map.255 = (bf16[1,2,1,64,1024]{4,3,2,1,0:T(8,128)(2,1)}, bf16[1,2,1,64,1024]{4,3,2,1,0:T(8,128)(2,1)}, f32[1,3,1024,128]{3,2,1,0:T(8,128)}, f32[1,2,128]{...) custom-call(bf16[2,64,1024]{2,1,0:T(8,128)(2,1)} %get-tuple-element., ...), custom_call_target="tpu_custom_call" | custom-call | tf_op jit(solution)/shard_map/pallas_call | solution.py:967
